TPU v7x, 32 devices: a whole 2x2x4 slice. The times are simulated.
32 devices in a mesh: tm: 8 (over z, y), chan: 4 (over x, core).
Axes of the slice: x: 2, y: 2, z: 4, core: 2. Of those that a mesh axis runs over, the one named last changes fastest.
Arguments:
- series: bfloat16 [2048, 512], P('tm', 'chan'), may hold values from -6 to 6
- proj_weight: bfloat16 [512, 3, 512], P(None, None, 'chan'), may hold values from -0.25 to 0.25
- proj_bias: float32 [3, 512], P(None, 'chan'), may hold values from -6 to 6
- short_taps: float32 [3, 3, 512], P(None, None, 'chan'), may hold values from -6 to 6
- short_bias: float32 [3, 512], P(None, 'chan'), may hold values from -6 to 6
- spectrum: float32 [2, 8, 2, 256, 512], P(None, 'tm', None, None, 'chan'), may hold values from -6 to 6
- skip_gain: float32 [512], P('chan'), may hold values from -6 to 6
- out_weight: bfloat16 [512, 512], replicated, may hold values from -0.25 to 0.25
- out_bias: float32 [512], P('chan'), may hold values from -6 to 6
Outputs:
- mixed_out: bfloat16 [2048, 512], P('tm', 'chan')
All inputs are finite; a program needn't handle non-finite values.
Results may differ from a plain program's by a relative error of at most 0.009.
Values may be sent and summed in bfloat16 or wider, within the bound.
A program may use at most 64 MiB of HBM per device.

v0:
```python
import math

import jax
import jax.numpy as jnp
from jax import lax
from jax.sharding import PartitionSpec as P


def from_behind(array, axis, by):
    length = lax.axis_size(axis)
    pairs = [(i, i + by) for i in range(length) if 0 <= i + by < length]
    return lax.ppermute(array, axis, pairs)


def partner_2(block, axis, bit):
    count = lax.axis_size(axis)
    route = []
    for low in range(count):
        high = low | 1 << bit
        if high != low and high < count:
            route += [(low, high), (high, low)]
    return lax.ppermute(block, axis, route)


def reverse_bits(values, digits):
    result = jnp.zeros_like(values)
    for bit_level in range(digits):
        result = result | (values >> bit_level & 1) << digits - 1 - bit_level
    return result


def turning(numer, denom):
    angle = numer.astype(jnp.float32) * (-2.0 * math.pi / denom)
    return (jnp.cos(angle), jnp.sin(angle))


def complex_times(stacked, real_part, imag_part):
    return jnp.stack(
        [
            stacked[0] * real_part - stacked[1] * imag_part,
            stacked[0] * imag_part + stacked[1] * real_part,
        ]
    )


def dft_rows(signals, period, inverse):
    indices = jnp.arange(period, dtype=jnp.int32)
    cosine, sine_part = turning(indices[:, None] * indices[None, :] % period, period)
    if inverse:
        sine_part = -sine_part
    stacked = jnp.concatenate([cosine, sine_part], 0)
    result = jnp.einsum("bt,retc->rebc", stacked, signals, precision=lax.Precision.HIGHEST)
    real_out = result[0, :, :period] - result[1, :, period:]
    imag_out = result[1, :, :period] + result[0, :, period:]
    return jnp.stack([real_out, imag_out])


def shards(
    series,
    proj_weight,
    proj_bias,
    short_taps,
    short_bias,
    spectrum,
    skip_gain,
    out_weight,
    out_bias,
):
    steps_dev = series.shape[0]
    model_width = proj_weight.shape[0]
    channels = proj_weight.shape[2]
    flat_weight = proj_weight.reshape(model_width, 3 * channels)
    weight_rows = flat_weight
    projected = jnp.dot(
        lax.all_gather(series, "chan", axis=1, tiled=True),
        weight_rows,
        preferred_element_type=jnp.float32,
    )
    projected = (projected.reshape(steps_dev, 3, channels) + proj_bias).astype(jnp.bfloat16)
    taps_count = short_taps.shape[0]
    earlier = from_behind(projected[steps_dev - taps_count + 1 :], "tm", 1)
    extended = jnp.concatenate([earlier, projected], 0).astype(jnp.float32)
    streams = short_bias + short_taps[0] * extended[taps_count - 1 :]
    for offset in range(1, taps_count):
        streams = (
            streams
            + short_taps[offset]
            * extended[taps_count - 1 - offset : taps_count - 1 - offset + steps_dev]
        )
    streams = lax.optimization_barrier(streams.astype(jnp.bfloat16)).astype(jnp.float32)
    gate_out = streams[:, 0]
    mixed_in = lax.optimization_barrier((streams[:, 1] * streams[:, 2]).astype(jnp.bfloat16))
    signal = mixed_in.astype(jnp.float32)
    tm_count = lax.axis_size("tm")
    digits = tm_count.bit_length() - 1
    own_index = lax.axis_index("tm")
    period = 2 * tm_count * steps_dev
    positions = jnp.arange(steps_dev, dtype=jnp.int32)
    own_rows = 2 * reverse_bits(own_index, digits) + jnp.arange(2, dtype=jnp.int32)
    twist_cos, twist_sin = turning(own_rows[:, None] * positions[None, :] % period, period)
    twist_cos, twist_sin = (twist_cos[:, :, None], twist_sin[:, :, None])
    half_cos, half_sin = turning(own_index, 2 * tm_count)
    zero_field = jnp.zeros_like(signal)
    current = jnp.stack(
        [jnp.stack([signal, signal * half_cos]), jnp.stack([zero_field, signal * half_sin])]
    )
    for bit_level in reversed(range(digits)):
        partner = partner_2(current, "tm", bit_level)
        half_span = 1 << bit_level
        rot_cos, rot_sin = turning(own_index % half_span, 2 * half_span)
        upper_half = own_index >> bit_level & 1 == 1
        current = jnp.where(
            upper_half, complex_times(partner - current, rot_cos, rot_sin), current + partner
        )
    twisted = complex_times(current, twist_cos, twist_sin)
    spectral = dft_rows(twisted, steps_dev, False)
    response = spectrum.reshape(2, 2, steps_dev, channels)
    product = complex_times(spectral, response[0], response[1])
    returned = dft_rows(product, steps_dev, True)
    current = complex_times(returned, twist_cos, -twist_sin)
    for bit_level in range(digits):
        partner = partner_2(current, "tm", bit_level)
        half_span = 1 << bit_level
        rot_cos, rot_sin = turning(own_index % half_span, 2 * half_span)
        rot_sin = -rot_sin
        upper_half = own_index >> bit_level & 1 == 1
        current = jnp.where(
            upper_half,
            partner - complex_times(current, rot_cos, rot_sin),
            current + complex_times(partner, rot_cos, rot_sin),
        )
    convolved = current[0, 0] + half_cos * current[0, 1] + half_sin * current[1, 1]
    convolved = convolved * (1.0 / period)
    gated_rows = ((convolved + skip_gain * signal) * gate_out).astype(jnp.bfloat16)
    column_start = lax.axis_index("chan") * channels
    weight_rows = lax.dynamic_slice_in_dim(out_weight, column_start, channels, 0)
    partial_value = jnp.dot(gated_rows, weight_rows, preferred_element_type=jnp.float32)
    mixed_out = lax.psum_scatter(partial_value, "chan", scatter_dimension=1, tiled=True)
    return (mixed_out + out_bias).astype(jnp.bfloat16)


def solution(mesh):
    return jax.shard_map(
        shards,
        mesh=mesh,
        in_specs=(
            P("tm", "chan"),
            P(None, None, "chan"),
            P(None, "chan"),
            P(None, None, "chan"),
            P(None, "chan"),
            P(None, "tm", None, None, "chan"),
            P("chan"),
            P(),
            P("chan"),
        ),
        out_specs=P("tm", "chan"),
        check_vma=False,
    )
```

profile of v0, /device:TPU:0, one launch (start us, length us, event | category | flops | bytes accessed | tf_op | source)
XLA Modules:
  0.0 162.2 jit_solution(7025656177095991762)
XLA Ops:
  6.5 1.2 copy.14
  7.8 7.2 %all_gather.3 = bf16[256,512]{1,0:T(8,128)(2,1)S(1)} all-gather(bf16[256,128]{1,0:T(8,128)(2,1)S(1)} %copy-done.6), channel_id=1, replica_groups=mesh['tm'=8,'chan'=4] {'chan'}, dimensions={1}, use_global_device_ids=true | all-gather | bytes 327680 | tf_op jit(solution)/shard_map/all_gather | solution.py:75
  15.0 0.3 fusion
  15.4 3.5 %collective-permute-start = (bf16[2,3,128]{2,0,1:T(2,128)(2,1)S(1)}, bf16[2,3,128]{2,0,1:T(2,128)(2,1)S(1)}, u32[]{:S(2)}, u32[]{:S(2)}) collective-permute-start(bf16[2,3,128]{2,0,1:T(2,128)(2,1)S(1)} %slice.184), channel_id=1, source_target_pairs={{0,4},{4,8},{8,12},{12,16},{16,20},{20,24},{24,28},{1,5},{5,9},{9,... | collective-permute-start | bytes 4616 | tf_op jit(solution)/shard_map/ppermute | solution.py:12
  19.0 1.1 collective-permute-done
  20.2 0.7 copy-done.9
  20.9 0.1 fusion.17
  21.1 0.6 copy-done.2
  21.8 4.3 %collective-permute-start.1 = (f32[2,2,256,128]{3,2,1,0:T(8,128)S(1)}, f32[2,2,256,128]{3,2,1,0:T(8,128)S(1)}, u32[]{:S(2)}, u32[]{:S(2)}) collective-permute-start(f32[2,2,256,128]{3,2,1,0:T(8,128)S(1)} %pad_maximum_fusion.2), channel_id=1, source_target_pairs={{0,16},{16,0},{4,20},{20,4},{8,24},{24,8},{12,28},{28,12},{1,17},{... | collective-permute-start | bytes 1572872 | tf_op jit(solution)/shard_map/ppermute | solution.py:22
  26.3 22.4 %collective-permute-done.1 = f32[2,2,256,128]{3,2,1,0:T(8,128)S(1)} collective-permute-done((f32[2,2,256,128]{3,2,1,0:T(8,128)S(1)}, f32[2,2,256,128]{3,2,1,0:T(8,128)S(1)}, u32[]{:S(2)}, u32[]{:S(2)}) %collective-permute-start.1) | collective-permute-done | bytes 524320 | tf_op jit(solution)/shard_map/ppermute | solution.py:22
  48.7 0.1 multiply_subtract_fusion.10
  48.8 0.9 maximum_select_fusion
  49.6 0.7 collective-permute-start.2
  50.5 1.1 fusion.62
  51.6 0.9 copy.23
  52.5 0.8 copy.24
  53.3 9.4 %collective-permute-done.2 = f32[2,2,256,128]{3,2,1,0:T(8,128)S(1)} collective-permute-done((f32[2,2,256,128]{3,2,1,0:T(8,128)}, f32[2,2,256,128]{3,2,1,0:T(8,128)S(1)}, u32[]{:S(2)}, u32[]{:S(2)}) %collective-permute-start.2) | collective-permute-done | bytes 524320 | tf_op jit(solution)/shard_map/ppermute | solution.py:22
  62.7 0.1 fusion.63
  62.8 0.1 multiply_subtract_fusion.9
  62.9 0.1 maximum_select_fusion.1
  63.0 0.7 collective-permute-start.3
  63.7 1.0 fusion.44
  64.7 1.0 fusion.42
  65.7 0.1 fusion.55
  65.8 9.6 %collective-permute-done.3 = f32[2,2,256,128]{3,2,1,0:T(8,128)S(1)} collective-permute-done((f32[2,2,256,128]{3,2,1,0:T(8,128)S(1)}, f32[2,2,256,128]{3,2,1,0:T(8,128)S(1)}, u32[]{:S(2)}, u32[]{:S(2)}) %collective-permute-start.3) | collective-permute-done | bytes 524320 | tf_op jit(solution)/shard_map/ppermute | solution.py:22
  75.5 0.1 maximum_select_fusion.2
  75.6 0.2 multiply_subtract_fusion.7
  75.8 1.9 %convolution_bitcast_fusion.1 = f32[2,2,512,128]{2,3,1,0:T(8,128)S(1)} fusion(f32[256,256]{1,0:T(8,128)S(1)} %get-tuple-element.41, f32[1,2,256,128]{3,2,1,0:T(8,128)S(1)} %get-tuple-element.11, f32[1,2,256,128]{3,2,1,0:T(8,128)S(1)} %get-tuple-element.10, f32[256,256]{1,0:T(8,128)S(1)} %get-tuple-element.40), kind=kOutput, calls=%fused_computation.1 | convolution fusion | flops 805568512 | bytes 2097152 | tf_op jit(solution)/shard_map/bt,retc->rebc/dot_general | solution.py:52
  77.7 0.1 fusion.24
  77.8 1.0 convolution_bitcast_fusion
  78.9 0.2 multiply_subtract_fusion.5
  79.1 0.7 collective-permute-start.4
  79.9 10.8 %collective-permute-done.4 = f32[2,2,256,128]{3,2,1,0:T(8,128)S(1)} collective-permute-done((f32[2,2,256,128]{3,2,1,0:T(8,128)S(1)}, f32[2,2,256,128]{3,2,1,0:T(8,128)S(1)}, u32[]{:S(2)}, u32[]{:S(2)}) %collective-permute-start.4) | collective-permute-done | bytes 524320 | tf_op jit(solution)/shard_map/ppermute | solution.py:22
  90.7 0.9 fusion.13
  91.6 3.0 %collective-permute-start.5 = (f32[2,2,256,128]{3,2,1,0:T(8,128)}, f32[2,2,256,128]{3,2,1,0:T(8,128)S(1)}, u32[]{:S(2)}, u32[]{:S(2)}) collective-permute-start(f32[2,2,256,128]{3,2,1,0:T(8,128)} %fusion.13), channel_id=1, source_target_pairs={{0,8},{8,0},{4,12},{12,4},{16,24},{24,16},{20,28},{28,20},{1,9},{9... | collective-permute-start | bytes 1572872 | tf_op jit(solution)/shard_map/ppermute | solution.py:22
  94.6 1.1 multiply_subtract_fusion.3
  95.7 8.5 %collective-permute-done.5 = f32[2,2,256,128]{3,2,1,0:T(8,128)S(1)} collective-permute-done((f32[2,2,256,128]{3,2,1,0:T(8,128)}, f32[2,2,256,128]{3,2,1,0:T(8,128)S(1)}, u32[]{:S(2)}, u32[]{:S(2)}) %collective-permute-start.5) | collective-permute-done | bytes 524320 | tf_op jit(solution)/shard_map/ppermute | solution.py:22
  104.2 0.1 multiply_subtract_fusion.2
  104.3 0.7 copy-done.1
  105.0 1.3 fusion.14
  106.3 4.4 %collective-permute-start.6 = (f32[2,2,256,128]{3,2,1,0:T(8,128)S(1)}, f32[2,2,256,128]{3,2,1,0:T(8,128)S(1)}, u32[]{:S(2)}, u32[]{:S(2)}) collective-permute-start(f32[2,2,256,128]{3,2,1,0:T(8,128)S(1)} %fusion.14), channel_id=1, source_target_pairs={{0,16},{16,0},{4,20},{20,4},{8,24},{24,8},{12,28},{28,12},{1,17},{... | collective-permute-start | bytes 1572872 | tf_op jit(solution)/shard_map/ppermute | solution.py:22
  110.8 19.9 %collective-permute-done.6 = f32[2,2,256,128]{3,2,1,0:T(8,128)S(1)} collective-permute-done((f32[2,2,256,128]{3,2,1,0:T(8,128)S(1)}, f32[2,2,256,128]{3,2,1,0:T(8,128)S(1)}, u32[]{:S(2)}, u32[]{:S(2)}) %collective-permute-start.6) | collective-permute-done | bytes 524320 | tf_op jit(solution)/shard_map/ppermute | solution.py:22
  130.6 0.1 multiply_subtract_fusion
  130.7 0.1 fusion.15
  130.8 0.7 copy-done.3
  131.5 1.0 fusion.40
  132.6 21.2 %reduce-scatter.2.cloned.1.call-done = f32[256,128]{1,0:T(8,128)} async-done(((f32[256,512]{1,0:T(8,128)}), f32[256,128]{1,0:T(8,128)}) %reduce-scatter.2.cloned.1.call-update) | async-done | bytes 131088 | tf_op jit(solution)/shard_map/reduce_scatter | solution.py:138
  153.8 1.5 add_convert_fusion
  (39 shorter events, 0.6 us)
Async XLA Ops:
  6.5 124.3 %copy-start = (bf16[512,512]{1,0:T(8,128)(2,1)S(1)}, bf16[512,512]{1,0:T(8,128)(2,1)}, u32[]{:S(2)}) copy-start(bf16[512,512]{1,0:T(8,128)(2,1)} %param.16) | copy-start | bytes 1572868
  6.5 1.2 copy-start.6
  6.5 147.3 %reduce-scatter.2.cloned.1.call-start = ((), (), s32[]{:S(2)}) async-start(), calls=%async_computation.1 | async-start | bytes 655360 | tf_op jit(solution)/shard_map/reduce_scatter | solution.py:138
  7.8 7.2 %copy-start.8 = (f32[3,128]{1,0:T(4,128)S(1)}, f32[3,128]{1,0:T(4,128)}, u32[]{:S(2)}) copy-start(f32[3,128]{1,0:T(4,128)} %param.11) | copy-start | bytes 4612
  15.0 3.8 %copy-start.7 = (f32[3,3,128]{2,1,0:T(4,128)S(1)}, f32[3,3,128]{2,1,0:T(4,128)}, u32[]{:S(2)}) copy-start(f32[3,3,128]{2,1,0:T(4,128)} %param.12) | copy-start | bytes 13828
  15.4 4.8 %collective-permute-start = (bf16[2,3,128]{2,0,1:T(2,128)(2,1)S(1)}, bf16[2,3,128]{2,0,1:T(2,128)(2,1)S(1)}, u32[]{:S(2)}, u32[]{:S(2)}) collective-permute-start(bf16[2,3,128]{2,0,1:T(2,128)(2,1)S(1)} %slice.184), channel_id=1, source_target_pairs={{0,4},{4,8},{8,12},{12,16},{16,20},{20,24},{24,28},{1,5},{5,9},{9,... | collective-permute-start | bytes 4616 | tf_op jit(solution)/shard_map/ppermute | solution.py:12
  20.2 0.7 copy-start.9
  21.1 0.6 copy-start.2
  21.8 26.8 %collective-permute-start.1 = (f32[2,2,256,128]{3,2,1,0:T(8,128)S(1)}, f32[2,2,256,128]{3,2,1,0:T(8,128)S(1)}, u32[]{:S(2)}, u32[]{:S(2)}) collective-permute-start(f32[2,2,256,128]{3,2,1,0:T(8,128)S(1)} %pad_maximum_fusion.2), channel_id=1, source_target_pairs={{0,16},{16,0},{4,20},{20,4},{8,24},{24,8},{12,28},{28,12},{1,17},{... | collective-permute-start | bytes 1572872 | tf_op jit(solution)/shard_map/ppermute | solution.py:22
  49.6 13.0 %collective-permute-start.2 = (f32[2,2,256,128]{3,2,1,0:T(8,128)}, f32[2,2,256,128]{3,2,1,0:T(8,128)S(1)}, u32[]{:S(2)}, u32[]{:S(2)}) collective-permute-start(f32[2,2,256,128]{3,2,1,0:T(8,128)} %maximum_select_fusion), channel_id=1, source_target_pairs={{0,8},{8,0},{4,12},{12,4},{16,24},{24,16},{20,28},{28,20},{1,9},{9... | collective-permute-start | bytes 1572872 | tf_op jit(solution)/shard_map/ppermute | solution.py:22
  63.0 12.4 %collective-permute-start.3 = (f32[2,2,256,128]{3,2,1,0:T(8,128)S(1)}, f32[2,2,256,128]{3,2,1,0:T(8,128)S(1)}, u32[]{:S(2)}, u32[]{:S(2)}) collective-permute-start(f32[2,2,256,128]{3,2,1,0:T(8,128)S(1)} %maximum_select_fusion.1), channel_id=1, source_target_pairs={{0,4},{4,0},{8,12},{12,8},{16,20},{20,16},{24,28},{28,24},{1,5},{5... | collective-permute-start | bytes 1572872 | tf_op jit(solution)/shard_map/ppermute | solution.py:22
  75.8 1.9 %copy-start.4 = (f32[1,1,2,256,128]{3,4,2,1,0:T(8,128)S(1)}, f32[1,1,2,256,128]{3,4,2,1,0:T(8,128)}, u32[]{:S(2)}) copy-start(f32[1,1,2,256,128]{3,4,2,1,0:T(8,128)} %copy.23) | copy-start | bytes 786436
  75.8 1.9 %copy-start.5 = (f32[1,1,2,256,128]{3,4,2,1,0:T(8,128)S(1)}, f32[1,1,2,256,128]{3,4,2,1,0:T(8,128)}, u32[]{:S(2)}) copy-start(f32[1,1,2,256,128]{3,4,2,1,0:T(8,128)} %copy.24) | copy-start | bytes 786436
  79.1 11.5 %collective-permute-start.4 = (f32[2,2,256,128]{3,2,1,0:T(8,128)S(1)}, f32[2,2,256,128]{3,2,1,0:T(8,128)S(1)}, u32[]{:S(2)}, u32[]{:S(2)}) collective-permute-start(f32[2,2,256,128]{3,2,1,0:T(8,128)S(1)} %pad_maximum_fusion.3), channel_id=1, source_target_pairs={{0,4},{4,0},{8,12},{12,8},{16,20},{20,16},{24,28},{28,24},{1,5},{5... | collective-permute-start | bytes 1572872 | tf_op jit(solution)/shard_map/ppermute | solution.py:22
  91.6 12.6 %collective-permute-start.5 = (f32[2,2,256,128]{3,2,1,0:T(8,128)}, f32[2,2,256,128]{3,2,1,0:T(8,128)S(1)}, u32[]{:S(2)}, u32[]{:S(2)}) collective-permute-start(f32[2,2,256,128]{3,2,1,0:T(8,128)} %fusion.13), channel_id=1, source_target_pairs={{0,8},{8,0},{4,12},{12,4},{16,24},{24,16},{20,28},{28,20},{1,9},{9... | collective-permute-start | bytes 1572872 | tf_op jit(solution)/shard_map/ppermute | solution.py:22
  104.2 0.8 copy-start.1
  106.3 24.3 %collective-permute-start.6 = (f32[2,2,256,128]{3,2,1,0:T(8,128)S(1)}, f32[2,2,256,128]{3,2,1,0:T(8,128)S(1)}, u32[]{:S(2)}, u32[]{:S(2)}) collective-permute-start(f32[2,2,256,128]{3,2,1,0:T(8,128)S(1)} %fusion.14), channel_id=1, source_target_pairs={{0,16},{16,0},{4,20},{20,4},{8,24},{24,8},{12,28},{28,12},{1,17},{... | collective-permute-start | bytes 1572872 | tf_op jit(solution)/shard_map/ppermute | solution.py:22
  130.7 0.8 copy-start.3
  130.7 0.8 copy-start.10
  132.6 21.2 %copy-start.11 = (f32[128]{0:T(128)S(1)}, f32[128]{0:T(128)}, u32[]{:S(2)}) copy-start(f32[128]{0:T(128)} %param.17) | copy-start | bytes 1540
Sparse Core Ops, SparseCore 0:
  132.7 21.0 reduce-scatter.1
where the time goes:
time: 163 us; the launch traced here: 162 us
  waiting for transfers between devices  103 us (63%)
  starting transfers between devices  17.3 us (11%)
  between operations  14.2 us (9%)
  other arithmetic  9.61 us (6%)
  blocking collectives  7.21 us (4%)
  local copies, waits for them, and re-layouts  6.76 us (4%)
  matrix products  4.23 us (3%)
    ppermute x6, waiting for transfers between devices, partner_2(): return lax.ppermute(block, axis, route)  80.5 us
    reduce_scatter x1, waiting for transfers between devices, shards(): lax.psum_scatter(partial_value, 'chan', scatter_dimension=1, tiled=True)  21.2 us
    ppermute x6, starting transfers between devices, partner_2(): return lax.ppermute(block, axis, route)  13.8 us
    all_gather x1, blocking collectives, shards(): lax.all_gather(series, 'chan', axis=1, tiled=True)  7.21 us
    unnamed x27, local copies, waits for them, and re-layouts  5.68 us
    ppermute x1, starting transfers between devices, from_behind(): return lax.ppermute(array, axis, pairs)  3.47 us
  transfers between devices with their start and end apart: 8, of which 8 were waited for; matrix products, arithmetic and copies ran while one was open for 4% of the time, Pallas kernels for 0%

commit v1 on v0

--- a/solution.py
+++ b/solution.py
@@ -1,9 +1,15 @@
+import functools
 import math
 
 import jax
 import jax.numpy as jnp
+import numpy as np
 from jax import lax
+from jax.experimental import pallas as pl
+from jax.experimental.pallas import tpu as pltpu
 from jax.sharding import PartitionSpec as P
+
+MESH = pl.DeviceIdType.MESH
 
 
 def from_behind(array, axis, by):
@@ -139,21 +145,409 @@
     return (mixed_out + out_bias).astype(jnp.bfloat16)
 
 
+def make_tables(tm_count, steps):
+    count, period = 2 * tm_count, 2 * tm_count * steps
+    rows = np.arange(steps)
+    angle = 2.0 * np.pi * (rows[:, None] * rows[None, :] % steps) / steps
+    dft = np.stack([np.cos(angle), np.sin(angle)]).astype(jnp.bfloat16)
+    angle = 2.0 * np.pi * (np.arange(count)[:, None] * rows[None, :] % period) / period
+    twist = np.stack([np.cos(angle), np.sin(angle)]).astype(np.float32)
+    return dft, twist
+
+
+def flip(value, digits):
+    result = 0
+    for bit_level in range(digits):
+        result |= (value >> bit_level & 1) << digits - 1 - bit_level
+    return result
+
+
+def weighted(blocks, weights):
+    total = None
+    for block, weight in zip(blocks, weights):
+        if abs(weight) < 1e-12:
+            continue
+        if abs(weight - 1.0) < 1e-12:
+            term = block
+        elif abs(weight + 1.0) < 1e-12:
+            term = -block
+        else:
+            term = block * float(weight)
+        total = term if total is None else total + term
+    return total
+
+
+def kernel(
+    tm_count,
+    chan_count,
+    series,
+    weight,
+    proj_bias,
+    taps,
+    short_bias,
+    spectrum,
+    skip_gain,
+    out_weight,
+    out_bias,
+    dft,
+    twist,
+    out,
+    rows_in,
+    weight_v,
+    proj_bias_v,
+    taps_v,
+    short_bias_v,
+    spectrum_v,
+    skip_v,
+    out_weight_v,
+    out_bias_v,
+    dft_v,
+    twist_v,
+    projected,
+    spec_out,
+    spec_in,
+    mixed_out,
+    mixed_in,
+    wave,
+    conv_out,
+    conv_in,
+    gated,
+    local_sem,
+    rows_send,
+    rows_recv,
+    halo_send,
+    halo_recv,
+    spec_send,
+    spec_recv,
+    mix_send,
+    mix_recv,
+    conv_send,
+    conv_recv,
+    gate_send,
+    gate_recv,
+):
+    steps, channels = series.shape
+    halo = rows_in.shape[0] - steps
+    share = channels // tm_count
+    digits = tm_count.bit_length() - 1
+    slots = 2 * tm_count
+    own_t, own_c = lax.axis_index("tm"), lax.axis_index("chan")
+    columns = lambda c: pl.ds(pl.multiple_of(c * channels, channels), channels)
+    tm_peer = lambda by: lax.rem(own_t + by, tm_count)
+    chan_peer = lambda by: lax.rem(own_c + by, chan_count)
+
+    barrier = pltpu.get_barrier_semaphore()
+    greet = lambda where: pl.semaphore_signal(barrier, inc=1, device_id=where, device_id_type=MESH)
+    for by in range(1, chan_count):
+        greet({"chan": chan_peer(by)})
+    for by in range(1, tm_count):
+        greet({"tm": tm_peer(by)})
+    for by in range(1, chan_count):
+        greet({"tm": tm_peer(1), "chan": chan_peer(by)})
+        greet({"tm": tm_peer(tm_count - 1), "chan": chan_peer(by)})
+
+    pairs = [
+        (spectrum.at[:, 0], spectrum_v),
+        (series, rows_in.at[pl.ds(halo, steps), columns(own_c)]),
+        (weight, weight_v),
+        (proj_bias, proj_bias_v),
+        (taps, taps_v),
+        (short_bias, short_bias_v),
+        (dft, dft_v),
+        (twist, twist_v),
+        (skip_gain, skip_v),
+        (out_weight.at[:, columns(own_c)], out_weight_v),
+        (out_bias, out_bias_v),
+    ]
+    local = [pltpu.make_async_copy(a, b, local_sem.at[i]) for i, (a, b) in enumerate(pairs)]
+    for copy in local:
+        copy.start()
+    pl.semaphore_wait(barrier, chan_count - 1 + tm_count - 1 + 2 * (chan_count - 1))
+
+    def remote(src, dst, send, recv, where):
+        return pltpu.make_async_remote_copy(
+            src_ref=src, dst_ref=dst, send_sem=send, recv_sem=recv, device_id=where, device_id_type=MESH
+        )
+
+    def rows_copy(by, owner):
+        return remote(
+            series,
+            rows_in.at[pl.ds(halo, steps), columns(owner)],
+            rows_send.at[by],
+            rows_recv.at[by],
+            {"chan": chan_peer(by)},
+        )
+
+    def halo_copy(by, owner):
+        return remote(
+            series.at[pl.ds(steps - halo, halo)],
+            rows_in.at[pl.ds(0, halo), columns(owner)],
+            halo_send.at[by],
+            halo_recv.at[by],
+            {"tm": tm_peer(1), "chan": chan_peer(by)},
+        )
+
+    for by in range(1, chan_count):
+        rows_copy(by, own_c).start()
+
+    @pl.when(own_t < tm_count - 1)
+    def _():
+        for by in range(chan_count):
+            halo_copy(by, own_c).start()
+
+    @pl.when(own_t == 0)
+    def _():
+        rows_in[pl.ds(0, halo), :] = jnp.zeros((halo, rows_in.shape[1]), rows_in.dtype)
+
+    local[0].wait()
+    for part in range(2):
+        for parity in range(2):
+            block = spectrum_v[part, parity].T * (1.0 / (slots * steps))
+            spec_out[:, part, parity] = block.astype(jnp.bfloat16).reshape(tm_count, share, steps)
+
+    def to_peer(src, dst, send, recv, by):
+        return remote(src.at[tm_peer(by)], dst.at[own_t], send.at[by], recv.at[by], {"tm": tm_peer(by)})
+
+    def spread(src, dst, send, recv):
+        for by in range(1, tm_count):
+            to_peer(src, dst, send, recv, by).start()
+        dst[own_t] = src[own_t]
+
+    def collect(src, dst, send, recv):
+        for by in range(1, tm_count):
+            copy = remote(
+                src.at[0], dst.at[tm_peer(tm_count - by)], send.at[by], recv.at[by], {"tm": tm_peer(by)}
+            )
+            copy.wait_recv()
+
+    spread(spec_out, spec_in, spec_send, spec_recv)
+
+    for copy in local[1:]:
+        copy.wait()
+    for by in range(1, chan_count):
+        rows_copy(by, chan_peer(chan_count - by)).wait_recv()
+
+    @pl.when(own_t > 0)
+    def _():
+        for by in range(chan_count):
+            halo_copy(by, chan_peer(chan_count - by)).wait_recv()
+
+    streams = []
+    for j in (1, 2, 0):
+        lanes = pl.ds(j * channels, channels)
+        value = jnp.dot(rows_in[...], weight_v[:, lanes], preferred_element_type=jnp.float32)
+        value = (value + proj_bias_v[j : j + 1]).astype(jnp.bfloat16).astype(jnp.float32)
+        projected[j] = value
+
+        @pl.when(own_t == 0)
+        def _():
+            projected[j, pl.ds(0, halo)] = jnp.zeros((halo, channels), jnp.float32)
+
+        stream = short_bias_v[j : j + 1] + taps_v[0, j : j + 1] * projected[j, pl.ds(halo, steps)]
+        for k in range(1, taps.shape[0]):
+            stream = stream + taps_v[k, j : j + 1] * projected[j, pl.ds(halo - k, steps)]
+        stream = stream.astype(jnp.bfloat16).astype(jnp.float32)
+        if j == 2:
+            signal = (streams[0] * stream).astype(jnp.bfloat16).astype(jnp.float32)
+            mixed_out[...] = signal.T.astype(jnp.bfloat16).reshape(tm_count, share, steps)
+            spread(mixed_out, mixed_in, mix_send, mix_recv)
+        streams.append(stream)
+    gate = streams[2]
+    projected[0, pl.ds(0, steps)] = gate
+    projected[1, pl.ds(0, steps)] = signal
+
+    collect(mixed_out, mixed_in, mix_send, mix_recv)
+    blocks = [mixed_in[b].astype(jnp.float32) for b in range(tm_count)]
+    turns = 2.0 * np.pi * np.arange(slots) / slots
+    cosine = lambda r, b: math.cos(turns[r * b % slots])
+    sine = lambda r, b: math.sin(turns[r * b % slots])
+    slot_of = {2 * flip(s // 2, digits) + s % 2: s for s in range(slots)}
+
+    for r in range(tm_count + 1):
+        real = weighted(blocks, [cosine(r, b) for b in range(tm_count)])
+        imag = weighted(blocks, [-sine(r, b) for b in range(tm_count)])
+        for to, sign in ((r, 1.0), (slots - r, -1.0)):
+            if to == slots or (sign < 0 and to == r):
+                continue
+            cos_row, sin_row = twist_v[0, to : to + 1], twist_v[1, to : to + 1]
+            if imag is None:
+                turned = (real * cos_row, -(real * sin_row))
+            else:
+                turned = (
+                    real * cos_row + sign * (imag * sin_row),
+                    sign * (imag * cos_row) - real * sin_row,
+                )
+            for part in range(2):
+                wave[part, slot_of[to]] = turned[part].astype(jnp.bfloat16)
+
+    def within():
+        rows = wave[...].reshape(2 * slots * share, steps)
+        first = jnp.dot(rows, dft_v[0], preferred_element_type=jnp.float32)
+        second = jnp.dot(rows, dft_v[1], preferred_element_type=jnp.float32)
+        half = slots * share
+        return first[:half], first[half:], second[:half], second[half:]
+
+    real_cos, imag_cos, real_sin, imag_sin = within()
+    real, imag = real_cos + imag_sin, imag_cos - real_sin
+    collect(spec_out, spec_in, spec_send, spec_recv)
+    filter_real = spec_in[:, 0].reshape(slots * share, steps).astype(jnp.float32)
+    filter_imag = spec_in[:, 1].reshape(slots * share, steps).astype(jnp.float32)
+    shape = (slots, share, steps)
+    wave[0] = (real * filter_real - imag * filter_imag).astype(jnp.bfloat16).reshape(shape)
+    wave[1] = (real * filter_imag + imag * filter_real).astype(jnp.bfloat16).reshape(shape)
+    real_cos, imag_cos, real_sin, imag_sin = within()
+    real, imag = (real_cos - imag_sin).reshape(shape), (real_sin + imag_cos).reshape(shape)
+
+    evens, odds = [], []
+    for r in range(tm_count + 1):
+        even = odd = None
+        for to, sign in ((r, 1.0), (slots - r, -1.0)):
+            if to == slots or (sign < 0 and to == r):
+                continue
+            s = slot_of[to]
+            cos_row, sin_row = twist_v[0, to : to + 1], twist_v[1, to : to + 1]
+            turned = real[s] * cos_row - imag[s] * sin_row
+            even = turned if even is None else even + turned
+            turned = real[s] * sin_row + imag[s] * cos_row
+            odd = turned if odd is None else odd - turned
+        evens.append(even)
+        odds.append(odd)
+    for b in range(tm_count):
+        weights = [cosine(r, b) for r in range(tm_count + 1)] + [-sine(r, b) for r in range(tm_count + 1)]
+        conv_out[b] = weighted(evens + odds, weights).astype(jnp.bfloat16)
+    spread(conv_out, conv_in, conv_send, conv_recv)
+    collect(conv_out, conv_in, conv_send, conv_recv)
+
+    convolved = conv_in[...].reshape(channels, steps).astype(jnp.float32).T
+    value = (convolved + skip_v[...] * projected[1, pl.ds(0, steps)]) * projected[0, pl.ds(0, steps)]
+    gated[:, columns(own_c)] = value.astype(jnp.bfloat16)
+
+    def gate_copy(by, owner):
+        return remote(
+            gated.at[:, columns(owner)],
+            gated.at[:, columns(owner)],
+            gate_send.at[by],
+            gate_recv.at[by],
+            {"chan": chan_peer(by)},
+        )
+
+    for by in range(1, chan_count):
+        gate_copy(by, own_c).start()
+    for by in range(1, chan_count):
+        gate_copy(by, chan_peer(chan_count - by)).wait_recv()
+    value = jnp.dot(gated[...], out_weight_v[...], preferred_element_type=jnp.float32)
+    out[...] = (value + out_bias_v[...]).astype(out.dtype)
+
+    for by in range(1, chan_count):
+        rows_copy(by, own_c).wait_send()
+        gate_copy(by, own_c).wait_send()
+
+    @pl.when(own_t < tm_count - 1)
+    def _():
+        for by in range(chan_count):
+            halo_copy(by, own_c).wait_send()
+
+    for by in range(1, tm_count):
+        to_peer(spec_out, spec_in, spec_send, spec_recv, by).wait_send()
+        to_peer(mixed_out, mixed_in, mix_send, mix_recv, by).wait_send()
+        to_peer(conv_out, conv_in, conv_send, conv_recv, by).wait_send()
+
+
+def fused(
+    series,
+    proj_weight,
+    proj_bias,
+    short_taps,
+    short_bias,
+    spectrum,
+    skip_gain,
+    out_weight,
+    out_bias,
+):
+    steps, channels = series.shape
+    width = proj_weight.shape[0]
+    tm_count, chan_count = lax.axis_size("tm"), lax.axis_size("chan")
+    dft, twist = make_tables(tm_count, steps)
+    share, slots, halo = channels // tm_count, 2 * tm_count, 16
+    spread_shape = (tm_count, share, steps)
+    vmem, dma = pltpu.VMEM, pltpu.SemaphoreType.DMA
+    operands = [
+        series,
+        proj_weight.reshape(width, 3 * channels),
+        proj_bias,
+        short_taps,
+        short_bias,
+        spectrum,
+        skip_gain.reshape(1, channels),
+        out_weight,
+        out_bias.reshape(1, channels),
+        jnp.asarray(dft),
+        jnp.asarray(twist),
+    ]
+    tm_sems = [dma((tm_count,)), dma((tm_count,))]
+    chan_sems = [dma((chan_count,)), dma((chan_count,))]
+    return pl.pallas_call(
+        functools.partial(kernel, tm_count, chan_count),
+        out_shape=jax.ShapeDtypeStruct((steps, channels), jnp.bfloat16),
+        in_specs=[pl.BlockSpec(memory_space=pl.ANY)] * len(operands),
+        out_specs=pl.BlockSpec(memory_space=pltpu.VMEM),
+        scratch_shapes=[
+            vmem((halo + steps, width), jnp.bfloat16),
+            vmem((width, 3 * channels), jnp.bfloat16),
+            vmem(proj_bias.shape, jnp.float32),
+            vmem(short_taps.shape, jnp.float32),
+            vmem(short_bias.shape, jnp.float32),
+            vmem((2, 2, steps, channels), jnp.float32),
+            vmem((1, channels), jnp.float32),
+            vmem((width, channels), jnp.bfloat16),
+            vmem((1, channels), jnp.float32),
+            vmem(dft.shape, jnp.bfloat16),
+            vmem(twist.shape, jnp.float32),
+            vmem((3, halo + steps, channels), jnp.float32),
+            vmem((tm_count, 2, 2, share, steps), jnp.bfloat16),
+            vmem((tm_count, 2, 2, share, steps), jnp.bfloat16),
+            vmem(spread_shape, jnp.bfloat16),
+            vmem(spread_shape, jnp.bfloat16),
+            vmem((2, slots, share, steps), jnp.bfloat16),
+            vmem(spread_shape, jnp.bfloat16),
+            vmem(spread_shape, jnp.bfloat16),
+            vmem((steps, width), jnp.bfloat16),
+            dma((len(operands),)),
+            *chan_sems,
+            *chan_sems,
+            *tm_sems,
+            *tm_sems,
+            *tm_sems,
+            *chan_sems,
+        ],
+        compiler_params=pltpu.CompilerParams(
+            collective_id=0, has_side_effects=True, vmem_limit_bytes=32 * 1024 * 1024
+        ),
+    )(*operands)
+
+
 def solution(mesh):
-    return jax.shard_map(
-        shards,
-        mesh=mesh,
-        in_specs=(
-            P("tm", "chan"),
-            P(None, None, "chan"),
-            P(None, "chan"),
-            P(None, None, "chan"),
-            P(None, "chan"),
-            P(None, "tm", None, None, "chan"),
-            P("chan"),
-            P(),
-            P("chan"),
-        ),
-        out_specs=P("tm", "chan"),
-        check_vma=False,
-    )
+    sizes = mesh.shape
+
+    def program(*arrays):
+        share = arrays[0].shape[1] // sizes["chan"] // sizes["tm"]
+        wide = share > 0 and share % 16 == 0 and sizes["tm"] >= 4
+        return jax.shard_map(
+            fused if wide else shards,
+            mesh=mesh,
+            in_specs=(
+                P("tm", "chan"),
+                P(None, None, "chan"),
+                P(None, "chan"),
+                P(None, None, "chan"),
+                P(None, "chan"),
+                P(None, "tm", None, None, "chan"),
+                P("chan"),
+                P(),
+                P("chan"),
+            ),
+            out_specs=P("tm", "chan"),
+            check_vma=False,
+        )(*arrays)
+
+    return program

time: 163 us -> 29.8 us (0.18)
  waiting for transfers between devices: 103 us -> 0 us
  Pallas kernels: 0 us -> 26.5 us
  starting transfers between devices: 17.3 us -> 0 us
  between operations: 14.2 us -> 0.12 us
  other arithmetic: 9.61 us -> 0 us
  blocking collectives: 7.21 us -> 0 us
  matrix products: 4.23 us -> 0 us
  local copies, waits for them, and re-layouts: 6.76 us -> 2.89 us
    ppermute x7 -> x0, waiting for transfers between devices: 81.6 us -> none  [the longest x6 80.5 us: partner_2(): return lax.ppermute(block, axis, route)]
    pallas_call x0 -> x1, Pallas kernels: none -> 26.5 us  [fused(): pl.pallas_call(functools.partial(kernel, tm_count, chan_count), out_shape...]
    reduce_scatter x1 -> x0, waiting for transfers between devices: 21.2 us -> none  [shards(): lax.psum_scatter(partial_value, 'chan', scatter_dimension=1, tiled=True)]
    ppermute x7 -> x0, starting transfers between devices: 17.3 us -> none  [the longest x6 13.8 us: partner_2(): return lax.ppermute(block, axis, route)]
    all_gather x1 -> x0, blocking collectives: 7.21 us -> none  [shards(): lax.all_gather(series, 'chan', axis=1, tiled=True)]
    dot_general x4 -> x0, matrix products: 4.23 us -> none  [the longest x2 2.89 us: dft_rows(): jnp.einsum('bt,retc->rebc', stacked, signals, precision=lax.Precision.HIG...]
    select_n x6 -> x0, other arithmetic: 3.35 us -> none  [the longest x3 2.27 us: shards(): jnp.where(upper_half, partner - complex_times(current, rot_cos, rot_sin),...]
    unnamed x27 -> x22, local copies, waits for them, and re-layouts: 5.68 us -> 2.68 us
  transfers between devices with their start and end apart: 8 -> 0, of which waited for: 8 -> 0; matrix products, arithmetic and copies ran while one was open for 4% -> 0% of each run, Pallas kernels for 0% -> 0%
where the time goes in v1:
time: 29.8 us; the launch traced here: 29.5 us
  Pallas kernels  26.5 us (89%)
  local copies, waits for them, and re-layouts  2.89 us (10%)
    pallas_call x1, Pallas kernels, fused(): pl.pallas_call(functools.partial(kernel, tm_count, chan_count), out_shape...  26.5 us
    unnamed x22, local copies, waits for them, and re-layouts  2.68 us

profile of v1, /device:TPU:0, one launch (start us, length us, event | category | flops | bytes accessed | tf_op | source)
XLA Modules:
  0.0 29.5 jit_solution(14407305032926125969)
XLA Ops:
  0.0 0.0 copy-start.1
  0.0 0.0 copy-start.3
  0.0 0.0 copy-start.4
  0.0 0.0 copy-start.5
  0.0 0.0 copy-start.6
  0.0 0.0 copy-start.7
  0.0 1.2 %copy.13 = bf16[512,3,128]{0,2,1:T(8,128)(2,1)S(1)} copy(bf16[512,3,128]{2,0,1:T(8,128)(2,1)} %param.12) | data formatting | bytes 786432 | tf_op args[1]
  1.3 0.0 copy-start
  1.3 0.0 copy-start.2
  1.3 0.0 copy-start.8
  1.3 0.0 copy-start.9
  1.3 0.2 copy.14.weight
  1.5 0.0 copy-done.1
  1.5 0.0 copy-done.3
  1.5 0.0 copy-done.4
  1.6 0.0 copy-done.5
  1.6 0.0 copy-done.6
  1.6 0.0 copy-done.7
  1.6 0.7 %copy-done = f32[2,1,2,256,128]{4,3,2,1,0:T(8,128)S(1)} copy-done((f32[2,1,2,256,128]{4,3,2,1,0:T(8,128)S(1)}, f32[2,1,2,256,128]{4,3,2,1,0:T(8,128)}, u32[]{:S(2)}) %copy-start) | copy-done | bytes 524312
  2.3 0.1 copy-done.2
  2.4 0.0 copy-done.8
  2.4 0.0 copy-done.9
  2.4 26.5 %shard_map.109 = bf16[256,128]{1,0:T(8,128)(2,1)S(1)} custom-call(bf16[256,128]{1,0:T(8,128)(2,1)S(1)} %copy-done.3, bf16[512,384]{1,0:T(8,128)(2,1)S(1)} %copy.14.weight, f32[3,128]{1,0:T(4,128)S(1)} %copy-done.6, f32[3,3,128]{2,1,0:T(4,128)S(1)} %copy-done.5, f32[3,128]{1,0:T(4,128)S(1)} %copy-done.7, f32[2,1,2,256,128]{4,3,2,1,0:T(8,128)S(1)} %copy-done, ...), custom_call_target="tpu_custom_call" | custom-call | tf_op jit(solution)/shard_map/pallas_call | solution.py:489
  28.9 0.6 %copy.16 = bf16[256,128]{1,0:T(8,128)(2,1)} copy(bf16[256,128]{1,0:T(8,128)(2,1)S(1)} %shard_map.109) | data formatting | bytes 131072
Async XLA Ops:
  0.0 1.5 %copy-start.1 = (bf16[512,512]{1,0:T(8,128)(2,1)S(1)}, bf16[512,512]{1,0:T(8,128)(2,1)}, u32[]{:S(2)}) copy-start(bf16[512,512]{1,0:T(8,128)(2,1)} %out_weight.1) | copy-start | bytes 1572868
  0.0 1.5 %copy-start.3 = (bf16[256,128]{1,0:T(8,128)(2,1)S(1)}, bf16[256,128]{1,0:T(8,128)(2,1)}, u32[]{:S(2)}) copy-start(bf16[256,128]{1,0:T(8,128)(2,1)} %series.1) | copy-start | bytes 196612
  0.0 1.5 %copy-start.4 = (f32[2,16,256]{2,1,0:T(8,128)S(1)}, f32[2,16,256]{2,1,0:T(8,128)}, u32[]{:S(2)}) copy-start(f32[2,16,256]{2,1,0:T(8,128)} %constant.5.clone.twist) | copy-start | bytes 98308
  0.0 1.5 %copy-start.5 = (f32[3,3,128]{2,1,0:T(4,128)S(1)}, f32[3,3,128]{2,1,0:T(4,128)}, u32[]{:S(2)}) copy-start(f32[3,3,128]{2,1,0:T(4,128)} %taps.1) | copy-start | bytes 13828
  0.0 1.6 %copy-start.6 = (f32[3,128]{1,0:T(4,128)S(1)}, f32[3,128]{1,0:T(4,128)}, u32[]{:S(2)}) copy-start(f32[3,128]{1,0:T(4,128)} %proj_bias.1) | copy-start | bytes 4612
  0.0 1.6 %copy-start.7 = (f32[3,128]{1,0:T(4,128)S(1)}, f32[3,128]{1,0:T(4,128)}, u32[]{:S(2)}) copy-start(f32[3,128]{1,0:T(4,128)} %short_bias.1) | copy-start | bytes 4612
  1.3 1.0 %copy-start = (f32[2,1,2,256,128]{4,3,2,1,0:T(8,128)S(1)}, f32[2,1,2,256,128]{4,3,2,1,0:T(8,128)}, u32[]{:S(2)}) copy-start(f32[2,1,2,256,128]{4,3,2,1,0:T(8,128)} %spectrum.1) | copy-start | bytes 1572868
  1.3 1.1 %copy-start.2 = (bf16[2,256,256]{2,1,0:T(8,128)(2,1)S(1)}, bf16[2,256,256]{2,1,0:T(8,128)(2,1)}, u32[]{:S(2)}) copy-start(bf16[2,256,256]{2,1,0:T(8,128)(2,1)} %constant.4.clone.dft) | copy-start | bytes 786436
  1.3 1.1 %copy-start.8 = (f32[128]{0:T(128)S(1)}, f32[128]{0:T(128)}, u32[]{:S(2)}) copy-start(f32[128]{0:T(128)} %param.17) | copy-start | bytes 1540
  1.3 1.1 %copy-start.9 = (f32[128]{0:T(128)S(1)}, f32[128]{0:T(128)}, u32[]{:S(2)}) copy-start(f32[128]{0:T(128)} %param.19) | copy-start | bytes 1540

commit v2 on v1

--- a/solution.py
+++ b/solution.py
@@ -200,6 +200,7 @@
     spectrum_v,
     skip_v,
     out_weight_v,
+    out_weight_t,
     out_bias_v,
     dft_v,
     twist_v,
@@ -211,6 +212,8 @@
     wave,
     conv_out,
     conv_in,
+    gate_t,
+    direct_t,
     gated,
     local_sem,
     rows_send,
@@ -247,8 +250,8 @@
         greet({"tm": tm_peer(tm_count - 1), "chan": chan_peer(by)})
 
     pairs = [
+        (series, rows_in.at[pl.ds(halo, steps), columns(own_c)]),
         (spectrum.at[:, 0], spectrum_v),
-        (series, rows_in.at[pl.ds(halo, steps), columns(own_c)]),
         (weight, weight_v),
         (proj_bias, proj_bias_v),
         (taps, taps_v),
@@ -262,6 +265,8 @@
     local = [pltpu.make_async_copy(a, b, local_sem.at[i]) for i, (a, b) in enumerate(pairs)]
     for copy in local:
         copy.start()
+    own_rows = rows_in.at[pl.ds(halo, steps), columns(own_c)]
+    local[0].wait()
     pl.semaphore_wait(barrier, chan_count - 1 + tm_count - 1 + 2 * (chan_count - 1))
 
     def remote(src, dst, send, recv, where):
@@ -271,7 +276,7 @@
 
     def rows_copy(by, owner):
         return remote(
-            series,
+            own_rows,
             rows_in.at[pl.ds(halo, steps), columns(owner)],
             rows_send.at[by],
             rows_recv.at[by],
@@ -280,7 +285,7 @@
 
     def halo_copy(by, owner):
         return remote(
-            series.at[pl.ds(steps - halo, halo)],
+            rows_in.at[pl.ds(steps, halo), columns(own_c)],
             rows_in.at[pl.ds(0, halo), columns(owner)],
             halo_send.at[by],
             halo_recv.at[by],
@@ -299,10 +304,16 @@
     def _():
         rows_in[pl.ds(0, halo), :] = jnp.zeros((halo, rows_in.shape[1]), rows_in.dtype)
 
-    local[0].wait()
-    for part in range(2):
-        for parity in range(2):
-            block = spectrum_v[part, parity].T * (1.0 / (slots * steps))
+    local[1].wait()
+    residue = 2 * sum((own_t >> i & 1) << digits - 1 - i for i in range(digits))
+    down = lax.broadcasted_iota(jnp.int32, (steps, steps), 0)
+    across = lax.broadcasted_iota(jnp.int32, (steps, steps), 1)
+    for parity in range(2):
+        wanted = jnp.where(residue + parity > tm_count, steps - 1 - down, down)
+        order = jnp.where(wanted == across, 1.0 / (slots * steps), 0.0).astype(jnp.bfloat16)
+        for part in range(2):
+            block = spectrum_v[part, parity].astype(jnp.bfloat16)
+            block = jnp.dot(order, block, preferred_element_type=jnp.float32).T
             spec_out[:, part, parity] = block.astype(jnp.bfloat16).reshape(tm_count, share, steps)
 
     def to_peer(src, dst, send, recv, by):
@@ -322,7 +333,7 @@
 
     spread(spec_out, spec_in, spec_send, spec_recv)
 
-    for copy in local[1:]:
+    for copy in local[2:]:
         copy.wait()
     for by in range(1, chan_count):
         rows_copy(by, chan_peer(chan_count - by)).wait_recv()
@@ -334,8 +345,7 @@
 
     streams = []
     for j in (1, 2, 0):
-        lanes = pl.ds(j * channels, channels)
-        value = jnp.dot(rows_in[...], weight_v[:, lanes], preferred_element_type=jnp.float32)
+        value = jnp.dot(rows_in[...], weight_v[j], preferred_element_type=jnp.float32)
         value = (value + proj_bias_v[j : j + 1]).astype(jnp.bfloat16).astype(jnp.float32)
         projected[j] = value
 
@@ -352,95 +362,96 @@
             mixed_out[...] = signal.T.astype(jnp.bfloat16).reshape(tm_count, share, steps)
             spread(mixed_out, mixed_in, mix_send, mix_recv)
         streams.append(stream)
-    gate = streams[2]
-    projected[0, pl.ds(0, steps)] = gate
-    projected[1, pl.ds(0, steps)] = signal
+    gate_t[...] = streams[2].T.reshape(tm_count, share, steps)
+    direct_t[...] = (skip_v[...] * signal).T.reshape(tm_count, share, steps)
+    for c in range(chan_count):
+        out_weight_t[c] = out_weight_v[pl.ds(c * channels, channels)].astype(jnp.float32).T.astype(jnp.bfloat16)
 
     collect(mixed_out, mixed_in, mix_send, mix_recv)
     blocks = [mixed_in[b].astype(jnp.float32) for b in range(tm_count)]
     turns = 2.0 * np.pi * np.arange(slots) / slots
     cosine = lambda r, b: math.cos(turns[r * b % slots])
     sine = lambda r, b: math.sin(turns[r * b % slots])
-    slot_of = {2 * flip(s // 2, digits) + s % 2: s for s in range(slots)}
-
-    for r in range(tm_count + 1):
+    kept = tm_count + 1
+
+    for r in range(kept):
         real = weighted(blocks, [cosine(r, b) for b in range(tm_count)])
         imag = weighted(blocks, [-sine(r, b) for b in range(tm_count)])
-        for to, sign in ((r, 1.0), (slots - r, -1.0)):
-            if to == slots or (sign < 0 and to == r):
-                continue
-            cos_row, sin_row = twist_v[0, to : to + 1], twist_v[1, to : to + 1]
-            if imag is None:
-                turned = (real * cos_row, -(real * sin_row))
-            else:
-                turned = (
-                    real * cos_row + sign * (imag * sin_row),
-                    sign * (imag * cos_row) - real * sin_row,
-                )
-            for part in range(2):
-                wave[part, slot_of[to]] = turned[part].astype(jnp.bfloat16)
+        cos_row, sin_row = twist_v[0, r : r + 1], twist_v[1, r : r + 1]
+        if imag is None:
+            turned = (real * cos_row, -(real * sin_row))
+        else:
+            turned = (real * cos_row + imag * sin_row, imag * cos_row - real * sin_row)
+        for part in range(2):
+            wave[part, r] = turned[part].astype(jnp.bfloat16)
 
     def within():
-        rows = wave[...].reshape(2 * slots * share, steps)
+        rows = wave[...].reshape(2 * kept * share, steps)
         first = jnp.dot(rows, dft_v[0], preferred_element_type=jnp.float32)
         second = jnp.dot(rows, dft_v[1], preferred_element_type=jnp.float32)
-        half = slots * share
-        return first[:half], first[half:], second[:half], second[half:]
+        half = kept * share
+        return [a.reshape(kept, share, steps) for a in (first[:half], first[half:], second[:half], second[half:])]
 
     real_cos, imag_cos, real_sin, imag_sin = within()
     real, imag = real_cos + imag_sin, imag_cos - real_sin
     collect(spec_out, spec_in, spec_send, spec_recv)
-    filter_real = spec_in[:, 0].reshape(slots * share, steps).astype(jnp.float32)
-    filter_imag = spec_in[:, 1].reshape(slots * share, steps).astype(jnp.float32)
-    shape = (slots, share, steps)
-    wave[0] = (real * filter_real - imag * filter_imag).astype(jnp.bfloat16).reshape(shape)
-    wave[1] = (real * filter_imag + imag * filter_real).astype(jnp.bfloat16).reshape(shape)
+
+    def filter_of(part, r):
+        return spec_in[flip(r // 2, digits), part, r % 2].astype(jnp.float32)
+
+    for r in range(kept):
+        filter_real, filter_imag = filter_of(0, r), filter_of(1, r)
+        if 0 < r < tm_count:
+            filter_real = filter_real + filter_of(0, slots - r)
+            filter_imag = filter_imag - filter_of(1, slots - r)
+        wave[0, r] = (real[r] * filter_real - imag[r] * filter_imag).astype(jnp.bfloat16)
+        wave[1, r] = (real[r] * filter_imag + imag[r] * filter_real).astype(jnp.bfloat16)
     real_cos, imag_cos, real_sin, imag_sin = within()
-    real, imag = (real_cos - imag_sin).reshape(shape), (real_sin + imag_cos).reshape(shape)
-
-    evens, odds = [], []
-    for r in range(tm_count + 1):
-        even = odd = None
-        for to, sign in ((r, 1.0), (slots - r, -1.0)):
-            if to == slots or (sign < 0 and to == r):
-                continue
-            s = slot_of[to]
-            cos_row, sin_row = twist_v[0, to : to + 1], twist_v[1, to : to + 1]
-            turned = real[s] * cos_row - imag[s] * sin_row
-            even = turned if even is None else even + turned
-            turned = real[s] * sin_row + imag[s] * cos_row
-            odd = turned if odd is None else odd - turned
-        evens.append(even)
-        odds.append(odd)
+    real, imag = real_cos - imag_sin, real_sin + imag_cos
+
+    terms = []
+    for r in range(kept):
+        cos_row, sin_row = twist_v[0, r : r + 1], twist_v[1, r : r + 1]
+        terms.append(real[r] * cos_row - imag[r] * sin_row)
+    for r in range(kept):
+        cos_row, sin_row = twist_v[0, r : r + 1], twist_v[1, r : r + 1]
+        terms.append(real[r] * sin_row + imag[r] * cos_row)
     for b in range(tm_count):
-        weights = [cosine(r, b) for r in range(tm_count + 1)] + [-sine(r, b) for r in range(tm_count + 1)]
-        conv_out[b] = weighted(evens + odds, weights).astype(jnp.bfloat16)
+        weights = [cosine(r, b) for r in range(kept)] + [-sine(r, b) for r in range(kept)]
+        conv_out[b] = weighted(terms, weights).astype(jnp.bfloat16)
     spread(conv_out, conv_in, conv_send, conv_recv)
-    collect(conv_out, conv_in, conv_send, conv_recv)
-
-    convolved = conv_in[...].reshape(channels, steps).astype(jnp.float32).T
-    value = (convolved + skip_v[...] * projected[1, pl.ds(0, steps)]) * projected[0, pl.ds(0, steps)]
-    gated[:, columns(own_c)] = value.astype(jnp.bfloat16)
-
-    def gate_copy(by, owner):
-        return remote(
-            gated.at[:, columns(owner)],
-            gated.at[:, columns(owner)],
-            gate_send.at[by],
-            gate_recv.at[by],
-            {"chan": chan_peer(by)},
-        )
-
-    for by in range(1, chan_count):
-        gate_copy(by, own_c).start()
-    for by in range(1, chan_count):
-        gate_copy(by, chan_peer(chan_count - by)).wait_recv()
-    value = jnp.dot(gated[...], out_weight_v[...], preferred_element_type=jnp.float32)
-    out[...] = (value + out_bias_v[...]).astype(out.dtype)
+
+    def gate_copy(by, owner, shift):
+        block = gated.at[owner, tm_peer(tm_count - shift)]
+        return remote(block, block, gate_send.at[by, shift], gate_recv.at[by, shift], {"chan": chan_peer(by)})
+
+    nearest = sorted(range(tm_count), key=lambda by: min(by, tm_count - by))
+    for shift in nearest:
+        source = tm_peer(tm_count - shift)
+        if shift:
+            remote(
+                conv_out.at[0], conv_in.at[source], conv_send.at[shift], conv_recv.at[shift], {"tm": tm_peer(shift)}
+            ).wait_recv()
+        value = (conv_in[source].astype(jnp.float32) + direct_t[source]) * gate_t[source]
+        gated[own_c, source] = value.astype(jnp.bfloat16)
+        for by in range(1, chan_count):
+            gate_copy(by, own_c, shift).start()
+
+    total = None
+    for by in range(chan_count):
+        owner = chan_peer(chan_count - by)
+        if by:
+            for shift in nearest:
+                gate_copy(by, owner, shift).wait_recv()
+        rows = gated[owner].reshape(channels, steps)
+        term = jnp.dot(out_weight_t[owner], rows, preferred_element_type=jnp.float32)
+        total = term if total is None else total + term
+    out[...] = (total.T + out_bias_v[...]).astype(out.dtype)
 
     for by in range(1, chan_count):
         rows_copy(by, own_c).wait_send()
-        gate_copy(by, own_c).wait_send()
+        for shift in nearest:
+            gate_copy(by, own_c, shift).wait_send()
 
     @pl.when(own_t < tm_count - 1)
     def _():
@@ -473,7 +484,7 @@
     vmem, dma = pltpu.VMEM, pltpu.SemaphoreType.DMA
     operands = [
         series,
-        proj_weight.reshape(width, 3 * channels),
+        proj_weight.transpose(1, 0, 2),
         proj_bias,
         short_taps,
         short_bias,
@@ -493,13 +504,14 @@
         out_specs=pl.BlockSpec(memory_space=pltpu.VMEM),
         scratch_shapes=[
             vmem((halo + steps, width), jnp.bfloat16),
-            vmem((width, 3 * channels), jnp.bfloat16),
+            vmem((3, width, channels), jnp.bfloat16),
             vmem(proj_bias.shape, jnp.float32),
             vmem(short_taps.shape, jnp.float32),
             vmem(short_bias.shape, jnp.float32),
             vmem((2, 2, steps, channels), jnp.float32),
             vmem((1, channels), jnp.float32),
             vmem((width, channels), jnp.bfloat16),
+            vmem((chan_count, channels, channels), jnp.bfloat16),
             vmem((1, channels), jnp.float32),
             vmem(dft.shape, jnp.bfloat16),
             vmem(twist.shape, jnp.float32),
@@ -508,20 +520,23 @@
             vmem((tm_count, 2, 2, share, steps), jnp.bfloat16),
             vmem(spread_shape, jnp.bfloat16),
             vmem(spread_shape, jnp.bfloat16),
-            vmem((2, slots, share, steps), jnp.bfloat16),
+            vmem((2, tm_count + 1, share, steps), jnp.bfloat16),
             vmem(spread_shape, jnp.bfloat16),
             vmem(spread_shape, jnp.bfloat16),
-            vmem((steps, width), jnp.bfloat16),
+            vmem(spread_shape, jnp.float32),
+            vmem(spread_shape, jnp.float32),
+            vmem((chan_count, *spread_shape), jnp.bfloat16),
             dma((len(operands),)),
             *chan_sems,
             *chan_sems,
             *tm_sems,
             *tm_sems,
             *tm_sems,
-            *chan_sems,
+            dma((chan_count, tm_count)),
+            dma((chan_count, tm_count)),
         ],
         compiler_params=pltpu.CompilerParams(
-            collective_id=0, has_side_effects=True, vmem_limit_bytes=32 * 1024 * 1024
+            collective_id=0, has_side_effects=True, vmem_limit_bytes=60 * 1024 * 1024
         ),
     )(*operands)
 

time: 29.8 us -> 29.4 us (0.987)
  local copies, waits for them, and re-layouts: 2.89 us -> 1.47 us
  Pallas kernels: 26.5 us -> 27.7 us
    pallas_call x1, Pallas kernels: 26.5 us -> 27.7 us  [fused(): pl.pallas_call(functools.partial(kernel, tm_count, chan_count), out_shape...]
    unnamed x22 -> x1, local copies, waits for them, and re-layouts: 2.68 us -> 1.47 us
where the time goes in v2:
time: 29.4 us; the launch traced here: 29.2 us
  Pallas kernels  27.7 us (94%)
  local copies, waits for them, and re-layouts  1.47 us (5%)
    pallas_call x1, Pallas kernels, fused(): pl.pallas_call(functools.partial(kernel, tm_count, chan_count), out_shape...  27.7 us
    unnamed x1, local copies, waits for them, and re-layouts  1.47 us

profile of v2, /device:TPU:0, one launch (start us, length us, event | category | flops | bytes accessed | tf_op | source)
XLA Modules:
  0.0 29.2 jit_solution(2813790037007547091)
XLA Ops:
  0.0 27.7 %shard_map.109 = bf16[256,128]{1,0:T(8,128)(2,1)} custom-call(bf16[256,128]{1,0:T(8,128)(2,1)} %series.1, bf16[3,512,128]{2,1,0:T(8,128)(2,1)} %bitcast.3, f32[3,128]{1,0:T(4,128)} %proj_bias.1, f32[3,3,128]{2,1,0:T(4,128)} %taps.1, f32[3,128]{1,0:T(4,128)} %short_bias.1, f32[2,1,2,256,128]{4,3,2,1,0:T(8,128)} %spectrum.1, f32[1,128]{1,0:T(1,128)} %bitcast.4, ...), custom_call_target="tpu_custom_call" | custom-call | tf_op jit(solution)/shard_map/pallas_call | solution.py:500
  27.8 1.5 %copy.13 = bf16[256,128]{1,0:T(8,128)(2,1)} copy(bf16[256,128]{1,0:T(8,128)(2,1)} %shard_map.109) | data formatting | bytes 131072

commit v3 on v2

--- a/solution.py
+++ b/solution.py
@@ -162,6 +162,15 @@
     return result
 
 
+def across_bits(index, by):
+    result, bit = index, 1
+    while bit <= by:
+        if by & bit:
+            result = result + bit * (1 - 2 * lax.rem(lax.div(index, bit), 2))
+        bit *= 2
+    return result
+
+
 def weighted(blocks, weights):
     total = None
     for block, weight in zip(blocks, weights):
@@ -236,8 +245,10 @@
     slots = 2 * tm_count
     own_t, own_c = lax.axis_index("tm"), lax.axis_index("chan")
     columns = lambda c: pl.ds(pl.multiple_of(c * channels, channels), channels)
-    tm_peer = lambda by: lax.rem(own_t + by, tm_count)
-    chan_peer = lambda by: lax.rem(own_c + by, chan_count)
+    next_t, last_t = lax.rem(own_t + 1, tm_count), lax.rem(own_t + tm_count - 1, tm_count)
+    tm_peer = lambda by: across_bits(own_t, by)
+    chan_peer = lambda by: across_bits(own_c, by)
+    far_first = list(range(tm_count // 2, tm_count)) + list(range(1, tm_count // 2))
 
     barrier = pltpu.get_barrier_semaphore()
     greet = lambda where: pl.semaphore_signal(barrier, inc=1, device_id=where, device_id_type=MESH)
@@ -246,8 +257,8 @@
     for by in range(1, tm_count):
         greet({"tm": tm_peer(by)})
     for by in range(1, chan_count):
-        greet({"tm": tm_peer(1), "chan": chan_peer(by)})
-        greet({"tm": tm_peer(tm_count - 1), "chan": chan_peer(by)})
+        greet({"tm": next_t, "chan": chan_peer(by)})
+        greet({"tm": last_t, "chan": chan_peer(by)})
 
     pairs = [
         (series, rows_in.at[pl.ds(halo, steps), columns(own_c)]),
@@ -266,43 +277,11 @@
     for copy in local:
         copy.start()
     own_rows = rows_in.at[pl.ds(halo, steps), columns(own_c)]
-    local[0].wait()
-    pl.semaphore_wait(barrier, chan_count - 1 + tm_count - 1 + 2 * (chan_count - 1))
 
     def remote(src, dst, send, recv, where):
         return pltpu.make_async_remote_copy(
             src_ref=src, dst_ref=dst, send_sem=send, recv_sem=recv, device_id=where, device_id_type=MESH
         )
-
-    def rows_copy(by, owner):
-        return remote(
-            own_rows,
-            rows_in.at[pl.ds(halo, steps), columns(owner)],
-            rows_send.at[by],
-            rows_recv.at[by],
-            {"chan": chan_peer(by)},
-        )
-
-    def halo_copy(by, owner):
-        return remote(
-            rows_in.at[pl.ds(steps, halo), columns(own_c)],
-            rows_in.at[pl.ds(0, halo), columns(owner)],
-            halo_send.at[by],
-            halo_recv.at[by],
-            {"tm": tm_peer(1), "chan": chan_peer(by)},
-        )
-
-    for by in range(1, chan_count):
-        rows_copy(by, own_c).start()
-
-    @pl.when(own_t < tm_count - 1)
-    def _():
-        for by in range(chan_count):
-            halo_copy(by, own_c).start()
-
-    @pl.when(own_t == 0)
-    def _():
-        rows_in[pl.ds(0, halo), :] = jnp.zeros((halo, rows_in.shape[1]), rows_in.dtype)
 
     local[1].wait()
     residue = 2 * sum((own_t >> i & 1) << digits - 1 - i for i in range(digits))
@@ -316,32 +295,60 @@
             block = jnp.dot(order, block, preferred_element_type=jnp.float32).T
             spec_out[:, part, parity] = block.astype(jnp.bfloat16).reshape(tm_count, share, steps)
 
-    def to_peer(src, dst, send, recv, by):
-        return remote(src.at[tm_peer(by)], dst.at[own_t], send.at[by], recv.at[by], {"tm": tm_peer(by)})
+    local[0].wait()
+    pl.semaphore_wait(barrier, chan_count - 1 + tm_count - 1 + 2 * (chan_count - 1))
+
+    def rows_copy(by, owner):
+        return remote(
+            own_rows,
+            rows_in.at[pl.ds(halo, steps), columns(owner)],
+            rows_send.at[0],
+            rows_recv.at[0],
+            {"chan": chan_peer(by)},
+        )
+
+    def halo_copy(by, owner):
+        return remote(
+            rows_in.at[pl.ds(steps, halo), columns(own_c)],
+            rows_in.at[pl.ds(0, halo), columns(owner)],
+            halo_send.at[0],
+            halo_recv.at[0],
+            {"tm": next_t, "chan": chan_peer(by)},
+        )
+
+    for by in range(1, chan_count):
+        rows_copy(by, own_c).start()
+
+    @pl.when(own_t < tm_count - 1)
+    def _():
+        for by in range(chan_count):
+            halo_copy(by, own_c).start()
+
+    @pl.when(own_t == 0)
+    def _():
+        rows_in[pl.ds(0, halo), :] = jnp.zeros((halo, rows_in.shape[1]), rows_in.dtype)
+
+    def bytes_of(ref, sem):
+        pltpu.make_async_copy(ref, ref, sem).wait()
 
     def spread(src, dst, send, recv):
-        for by in range(1, tm_count):
-            to_peer(src, dst, send, recv, by).start()
+        for by in far_first:
+            remote(src.at[tm_peer(by)], dst.at[own_t], send.at[0], recv.at[0], {"tm": tm_peer(by)}).start()
         dst[own_t] = src[own_t]
 
-    def collect(src, dst, send, recv):
-        for by in range(1, tm_count):
-            copy = remote(
-                src.at[0], dst.at[tm_peer(tm_count - by)], send.at[by], recv.at[by], {"tm": tm_peer(by)}
-            )
-            copy.wait_recv()
+    def collect(dst, recv):
+        bytes_of(dst.at[pl.ds(0, tm_count - 1)], recv.at[0])
 
     spread(spec_out, spec_in, spec_send, spec_recv)
 
     for copy in local[2:]:
         copy.wait()
-    for by in range(1, chan_count):
-        rows_copy(by, chan_peer(chan_count - by)).wait_recv()
+    others = pl.ds(0, (chan_count - 1) * channels)
+    bytes_of(rows_in.at[pl.ds(halo, steps), others], rows_recv.at[0])
 
     @pl.when(own_t > 0)
     def _():
-        for by in range(chan_count):
-            halo_copy(by, chan_peer(chan_count - by)).wait_recv()
+        bytes_of(rows_in.at[pl.ds(0, halo)], halo_recv.at[0])
 
     streams = []
     for j in (1, 2, 0):
@@ -365,9 +372,15 @@
     gate_t[...] = streams[2].T.reshape(tm_count, share, steps)
     direct_t[...] = (skip_v[...] * signal).T.reshape(tm_count, share, steps)
     for c in range(chan_count):
-        out_weight_t[c] = out_weight_v[pl.ds(c * channels, channels)].astype(jnp.float32).T.astype(jnp.bfloat16)
-
-    collect(mixed_out, mixed_in, mix_send, mix_recv)
+        blocks = [
+            out_weight_v[pl.ds(pl.multiple_of(c * channels + tm_peer(by) * share, share), share)]
+            for by in range(tm_count)
+        ]
+        turned = jnp.concatenate(blocks, 0).astype(jnp.float32).T.astype(jnp.bfloat16)
+        out_weight_t[0, c] = turned[:, : channels // 2]
+        out_weight_t[1, c] = turned[:, channels // 2 :]
+
+    collect(mixed_in, mix_recv)
     blocks = [mixed_in[b].astype(jnp.float32) for b in range(tm_count)]
     turns = 2.0 * np.pi * np.arange(slots) / slots
     cosine = lambda r, b: math.cos(turns[r * b % slots])
@@ -394,7 +407,7 @@
 
     real_cos, imag_cos, real_sin, imag_sin = within()
     real, imag = real_cos + imag_sin, imag_cos - real_sin
-    collect(spec_out, spec_in, spec_send, spec_recv)
+    collect(spec_in, spec_recv)
 
     def filter_of(part, r):
         return spec_in[flip(r // 2, digits), part, r % 2].astype(jnp.float32)
@@ -419,49 +432,47 @@
     for b in range(tm_count):
         weights = [cosine(r, b) for r in range(kept)] + [-sine(r, b) for r in range(kept)]
         conv_out[b] = weighted(terms, weights).astype(jnp.bfloat16)
-    spread(conv_out, conv_in, conv_send, conv_recv)
-
-    def gate_copy(by, owner, shift):
-        block = gated.at[owner, tm_peer(tm_count - shift)]
-        return remote(block, block, gate_send.at[by, shift], gate_recv.at[by, shift], {"chan": chan_peer(by)})
-
-    nearest = sorted(range(tm_count), key=lambda by: min(by, tm_count - by))
-    for shift in nearest:
-        source = tm_peer(tm_count - shift)
-        if shift:
-            remote(
-                conv_out.at[0], conv_in.at[source], conv_send.at[shift], conv_recv.at[shift], {"tm": tm_peer(shift)}
-            ).wait_recv()
-        value = (conv_in[source].astype(jnp.float32) + direct_t[source]) * gate_t[source]
-        gated[own_c, source] = value.astype(jnp.bfloat16)
-        for by in range(1, chan_count):
-            gate_copy(by, own_c, shift).start()
-
-    total = None
-    for by in range(chan_count):
-        owner = chan_peer(chan_count - by)
-        if by:
-            for shift in nearest:
-                gate_copy(by, owner, shift).wait_recv()
-        rows = gated[owner].reshape(channels, steps)
-        term = jnp.dot(out_weight_t[owner], rows, preferred_element_type=jnp.float32)
-        total = term if total is None else total + term
-    out[...] = (total.T + out_bias_v[...]).astype(out.dtype)
-
-    for by in range(1, chan_count):
-        rows_copy(by, own_c).wait_send()
-        for shift in nearest:
-            gate_copy(by, own_c, shift).wait_send()
+    near = tm_count // 2
+    for by in far_first:
+        half = by // near
+        remote(
+            conv_out.at[tm_peer(by)], conv_in.at[by], conv_send.at[0], conv_recv.at[half], {"tm": tm_peer(by)}
+        ).start()
+
+    bytes_of(rows_in.at[pl.ds(halo, steps), others], rows_send.at[0])
 
     @pl.when(own_t < tm_count - 1)
     def _():
-        for by in range(chan_count):
-            halo_copy(by, own_c).wait_send()
-
-    for by in range(1, tm_count):
-        to_peer(spec_out, spec_in, spec_send, spec_recv, by).wait_send()
-        to_peer(mixed_out, mixed_in, mix_send, mix_recv, by).wait_send()
-        to_peer(conv_out, conv_in, conv_send, conv_recv, by).wait_send()
+        bytes_of(rows_in.at[pl.ds(0, halo)], halo_send.at[0])
+
+    bytes_of(spec_in.at[pl.ds(0, tm_count - 1)], spec_send.at[0])
+    bytes_of(mixed_in.at[pl.ds(0, tm_count - 1)], mix_send.at[0])
+
+    for half in range(2):
+        if half == 0:
+            bytes_of(conv_in.at[pl.ds(0, near - 1)], conv_recv.at[0])
+        else:
+            bytes_of(conv_in.at[pl.ds(0, near)], conv_recv.at[1])
+        for by in range(half * near, (half + 1) * near):
+            source = tm_peer(by)
+            arrived = conv_in[by] if by else conv_out[source]
+            value = (arrived.astype(jnp.float32) + direct_t[source]) * gate_t[source]
+            gated[half, own_c, pl.ds(by % near * share, share)] = value.astype(jnp.bfloat16)
+        for by in range(chan_count - 1, 0, -1):
+            block = gated.at[half, own_c]
+            remote(block, block, gate_send.at[half], gate_recv.at[half], {"chan": chan_peer(by)}).start()
+
+    total = None
+    for half in range(2):
+        bytes_of(gated.at[half, pl.ds(0, chan_count - 1)], gate_recv.at[half])
+        for c in range(chan_count):
+            term = jnp.dot(out_weight_t[half, c], gated[half, c], preferred_element_type=jnp.float32)
+            total = term if total is None else total + term
+    out[...] = (total.T + out_bias_v[...]).astype(out.dtype)
+
+    bytes_of(conv_in.at[pl.ds(0, tm_count - 1)], conv_send.at[0])
+    for half in range(2):
+        bytes_of(gated.at[half, pl.ds(0, chan_count - 1)], gate_send.at[half])
 
 
 def fused(
@@ -495,8 +506,6 @@
         jnp.asarray(dft),
         jnp.asarray(twist),
     ]
-    tm_sems = [dma((tm_count,)), dma((tm_count,))]
-    chan_sems = [dma((chan_count,)), dma((chan_count,))]
     return pl.pallas_call(
         functools.partial(kernel, tm_count, chan_count),
         out_shape=jax.ShapeDtypeStruct((steps, channels), jnp.bfloat16),
@@ -511,7 +520,7 @@
             vmem((2, 2, steps, channels), jnp.float32),
             vmem((1, channels), jnp.float32),
             vmem((width, channels), jnp.bfloat16),
-            vmem((chan_count, channels, channels), jnp.bfloat16),
+            vmem((2, chan_count, channels, channels // 2), jnp.bfloat16),
             vmem((1, channels), jnp.float32),
             vmem(dft.shape, jnp.bfloat16),
             vmem(twist.shape, jnp.float32),
@@ -525,15 +534,9 @@
             vmem(spread_shape, jnp.bfloat16),
             vmem(spread_shape, jnp.float32),
             vmem(spread_shape, jnp.float32),
-            vmem((chan_count, *spread_shape), jnp.bfloat16),
+            vmem((2, chan_count, channels // 2, steps), jnp.bfloat16),
             dma((len(operands),)),
-            *chan_sems,
-            *chan_sems,
-            *tm_sems,
-            *tm_sems,
-            *tm_sems,
-            dma((chan_count, tm_count)),
-            dma((chan_count, tm_count)),
+            *[dma((2,))] * 12,
         ],
         compiler_params=pltpu.CompilerParams(
             collective_id=0, has_side_effects=True, vmem_limit_bytes=60 * 1024 * 1024
@@ -547,6 +550,7 @@
     def program(*arrays):
         share = arrays[0].shape[1] // sizes["chan"] // sizes["tm"]
         wide = share > 0 and share % 16 == 0 and sizes["tm"] >= 4
+        wide = wide and all(size & size - 1 == 0 for size in sizes.values())
         return jax.shard_map(
             fused if wide else shards,
             mesh=mesh,

time: 29.4 us -> 28 us (0.952)
  Pallas kernels: 27.7 us -> 26.3 us
    pallas_call x1, Pallas kernels: 27.7 us -> 26.3 us  [fused(): pl.pallas_call(functools.partial(kernel, tm_count, chan_count), out_shape...]
where the time goes in v3:
time: 28 us; the launch traced here: 27.8 us
  Pallas kernels  26.3 us (94%)
  local copies, waits for them, and re-layouts  1.47 us (5%)
    pallas_call x1, Pallas kernels, fused(): pl.pallas_call(functools.partial(kernel, tm_count, chan_count), out_shape...  26.3 us
    unnamed x1, local copies, waits for them, and re-layouts  1.47 us

profile of v3, /device:TPU:0, one launch (start us, length us, event | category | flops | bytes accessed | tf_op | source)
XLA Modules:
  0.0 27.8 jit_solution(7914848172213971519)
XLA Ops:
  0.0 26.3 %shard_map.109 = bf16[256,128]{1,0:T(8,128)(2,1)} custom-call(bf16[256,128]{1,0:T(8,128)(2,1)} %series.1, bf16[3,512,128]{2,1,0:T(8,128)(2,1)} %bitcast.3, f32[3,128]{1,0:T(4,128)} %proj_bias.1, f32[3,3,128]{2,1,0:T(4,128)} %taps.1, f32[3,128]{1,0:T(4,128)} %short_bias.1, f32[2,1,2,256,128]{4,3,2,1,0:T(8,128)} %spectrum.1, f32[1,128]{1,0:T(1,128)} %bitcast.4, ...), custom_call_target="tpu_custom_call" | custom-call | tf_op jit(solution)/shard_map/pallas_call | solution.py:509
  26.3 1.5 %copy.13 = bf16[256,128]{1,0:T(8,128)(2,1)} copy(bf16[256,128]{1,0:T(8,128)(2,1)} %shard_map.109) | data formatting | bytes 131072

commit v4 on v3

--- a/solution.py
+++ b/solution.py
@@ -263,7 +263,7 @@
     pairs = [
         (series, rows_in.at[pl.ds(halo, steps), columns(own_c)]),
         (spectrum.at[:, 0], spectrum_v),
-        (weight, weight_v),
+        *[(weight.at[j], weight_v.at[:, pl.ds(j * channels, channels)]) for j in range(3)],
         (proj_bias, proj_bias_v),
         (taps, taps_v),
         (short_bias, short_bias_v),
@@ -283,29 +283,29 @@
             src_ref=src, dst_ref=dst, send_sem=send, recv_sem=recv, device_id=where, device_id_type=MESH
         )
 
-    local[1].wait()
     residue = 2 * sum((own_t >> i & 1) << digits - 1 - i for i in range(digits))
     down = lax.broadcasted_iota(jnp.int32, (steps, steps), 0)
     across = lax.broadcasted_iota(jnp.int32, (steps, steps), 1)
-    for parity in range(2):
+
+    def turn_spectrum(parity):
         wanted = jnp.where(residue + parity > tm_count, steps - 1 - down, down)
         order = jnp.where(wanted == across, 1.0 / (slots * steps), 0.0).astype(jnp.bfloat16)
         for part in range(2):
             block = spectrum_v[part, parity].astype(jnp.bfloat16)
             block = jnp.dot(order, block, preferred_element_type=jnp.float32).T
-            spec_out[:, part, parity] = block.astype(jnp.bfloat16).reshape(tm_count, share, steps)
-
+            spec_out[parity, :, part] = block.astype(jnp.bfloat16).reshape(tm_count, share, steps)
+
+    local[1].wait()
+    turn_spectrum(0)
     local[0].wait()
     pl.semaphore_wait(barrier, chan_count - 1 + tm_count - 1 + 2 * (chan_count - 1))
 
-    def rows_copy(by, owner):
-        return remote(
-            own_rows,
-            rows_in.at[pl.ds(halo, steps), columns(owner)],
-            rows_send.at[0],
-            rows_recv.at[0],
-            {"chan": chan_peer(by)},
-        )
+    core_c, x_c, far_c = chan_peer(1), chan_peer(2), chan_peer(3)
+    part_rows = steps // 2
+
+    def rows_copy(owner, first, count, recv, to):
+        block = rows_in.at[pl.ds(halo + first, count), columns(owner)]
+        return remote(block, block, rows_send.at[0], rows_recv.at[recv], {"chan": to})
 
     def halo_copy(by, owner):
         return remote(
@@ -316,8 +316,9 @@
             {"tm": next_t, "chan": chan_peer(by)},
         )
 
-    for by in range(1, chan_count):
-        rows_copy(by, own_c).start()
+    for i in range(2):
+        rows_copy(own_c, i * part_rows, part_rows, i, x_c).start()
+    rows_copy(own_c, 0, steps, 2, core_c).start()
 
     @pl.when(own_t < tm_count - 1)
     def _():
@@ -333,26 +334,41 @@
 
     def spread(src, dst, send, recv):
         for by in far_first:
-            remote(src.at[tm_peer(by)], dst.at[own_t], send.at[0], recv.at[0], {"tm": tm_peer(by)}).start()
+            remote(src.at[tm_peer(by)], dst.at[own_t], send, recv, {"tm": tm_peer(by)}).start()
         dst[own_t] = src[own_t]
 
     def collect(dst, recv):
-        bytes_of(dst.at[pl.ds(0, tm_count - 1)], recv.at[0])
-
-    spread(spec_out, spec_in, spec_send, spec_recv)
-
+        bytes_of(dst.at[pl.ds(0, tm_count - 1)], recv)
+
+    spread(spec_out.at[0], spec_in.at[0], spec_send.at[0], spec_recv.at[0])
+    turn_spectrum(1)
+    spread(spec_out.at[1], spec_in.at[1], spec_send.at[1], spec_recv.at[1])
+
+    for i in range(2):
+        bytes_of(rows_in.at[pl.ds(halo, part_rows), columns(x_c)], rows_recv.at[i])
+        rows_copy(x_c, i * part_rows, part_rows, 3, core_c).start()
     for copy in local[2:]:
         copy.wait()
     others = pl.ds(0, (chan_count - 1) * channels)
-    bytes_of(rows_in.at[pl.ds(halo, steps), others], rows_recv.at[0])
 
     @pl.when(own_t > 0)
     def _():
         bytes_of(rows_in.at[pl.ds(0, halo)], halo_recv.at[0])
 
+    bytes_of(rows_in.at[pl.ds(halo, steps), columns(core_c)], rows_recv.at[2])
+
+    def of_chip(chip):
+        inputs = pl.ds(pl.multiple_of(chip * 2 * channels, 2 * channels), 2 * channels)
+        return jnp.dot(rows_in[:, inputs], weight_v[inputs, :], preferred_element_type=jnp.float32)
+
+    own_chip = lax.div(own_c, 2)
+    near_sum = of_chip(own_chip)
+    bytes_of(rows_in.at[pl.ds(halo, steps), columns(far_c)], rows_recv.at[3])
+    sums = near_sum + of_chip(1 - own_chip)
+
     streams = []
     for j in (1, 2, 0):
-        value = jnp.dot(rows_in[...], weight_v[j], preferred_element_type=jnp.float32)
+        value = sums[:, j * channels : (j + 1) * channels]
         value = (value + proj_bias_v[j : j + 1]).astype(jnp.bfloat16).astype(jnp.float32)
         projected[j] = value
 
@@ -367,20 +383,20 @@
         if j == 2:
             signal = (streams[0] * stream).astype(jnp.bfloat16).astype(jnp.float32)
             mixed_out[...] = signal.T.astype(jnp.bfloat16).reshape(tm_count, share, steps)
-            spread(mixed_out, mixed_in, mix_send, mix_recv)
+            spread(mixed_out, mixed_in, mix_send.at[0], mix_recv.at[0])
         streams.append(stream)
     gate_t[...] = streams[2].T.reshape(tm_count, share, steps)
     direct_t[...] = (skip_v[...] * signal).T.reshape(tm_count, share, steps)
-    for c in range(chan_count):
+    near = tm_count // 2
+    for half in range(2):
         blocks = [
-            out_weight_v[pl.ds(pl.multiple_of(c * channels + tm_peer(by) * share, share), share)]
-            for by in range(tm_count)
+            out_weight_v[pl.ds(pl.multiple_of(c * channels + tm_peer(half * near + by) * share, share), share)]
+            for c in range(chan_count)
+            for by in range(near)
         ]
-        turned = jnp.concatenate(blocks, 0).astype(jnp.float32).T.astype(jnp.bfloat16)
-        out_weight_t[0, c] = turned[:, : channels // 2]
-        out_weight_t[1, c] = turned[:, channels // 2 :]
-
-    collect(mixed_in, mix_recv)
+        out_weight_t[half] = jnp.concatenate(blocks, 0).astype(jnp.float32).T.astype(jnp.bfloat16)
+
+    collect(mixed_in, mix_recv.at[0])
     blocks = [mixed_in[b].astype(jnp.float32) for b in range(tm_count)]
     turns = 2.0 * np.pi * np.arange(slots) / slots
     cosine = lambda r, b: math.cos(turns[r * b % slots])
@@ -407,10 +423,11 @@
 
     real_cos, imag_cos, real_sin, imag_sin = within()
     real, imag = real_cos + imag_sin, imag_cos - real_sin
-    collect(spec_in, spec_recv)
+    for parity in range(2):
+        collect(spec_in.at[parity], spec_recv.at[parity])
 
     def filter_of(part, r):
-        return spec_in[flip(r // 2, digits), part, r % 2].astype(jnp.float32)
+        return spec_in[r % 2, flip(r // 2, digits), part].astype(jnp.float32)
 
     for r in range(kept):
         filter_real, filter_imag = filter_of(0, r), filter_of(1, r)
@@ -432,7 +449,6 @@
     for b in range(tm_count):
         weights = [cosine(r, b) for r in range(kept)] + [-sine(r, b) for r in range(kept)]
         conv_out[b] = weighted(terms, weights).astype(jnp.bfloat16)
-    near = tm_count // 2
     for by in far_first:
         half = by // near
         remote(
@@ -445,8 +461,13 @@
     def _():
         bytes_of(rows_in.at[pl.ds(0, halo)], halo_send.at[0])
 
-    bytes_of(spec_in.at[pl.ds(0, tm_count - 1)], spec_send.at[0])
+    for parity in range(2):
+        collect(spec_in.at[parity], spec_send.at[parity])
     bytes_of(mixed_in.at[pl.ds(0, tm_count - 1)], mix_send.at[0])
+
+    def gate_copy(half, owner, recv, to):
+        block = gated.at[half, owner]
+        return remote(block, block, gate_send.at[half], gate_recv.at[half, recv], {"chan": to})
 
     for half in range(2):
         if half == 0:
@@ -458,16 +479,19 @@
             arrived = conv_in[by] if by else conv_out[source]
             value = (arrived.astype(jnp.float32) + direct_t[source]) * gate_t[source]
             gated[half, own_c, pl.ds(by % near * share, share)] = value.astype(jnp.bfloat16)
-        for by in range(chan_count - 1, 0, -1):
-            block = gated.at[half, own_c]
-            remote(block, block, gate_send.at[half], gate_recv.at[half], {"chan": chan_peer(by)}).start()
+        gate_copy(half, own_c, 0, x_c).start()
+        gate_copy(half, own_c, 1, core_c).start()
+    for half in range(2):
+        bytes_of(gated.at[half, x_c], gate_recv.at[half, 0])
+        gate_copy(half, x_c, 2, core_c).start()
 
     total = None
     for half in range(2):
-        bytes_of(gated.at[half, pl.ds(0, chan_count - 1)], gate_recv.at[half])
-        for c in range(chan_count):
-            term = jnp.dot(out_weight_t[half, c], gated[half, c], preferred_element_type=jnp.float32)
-            total = term if total is None else total + term
+        bytes_of(gated.at[half, core_c], gate_recv.at[half, 1])
+        bytes_of(gated.at[half, far_c], gate_recv.at[half, 2])
+        rows = gated[half].reshape(chan_count * channels // 2, steps)
+        term = jnp.dot(out_weight_t[half], rows, preferred_element_type=jnp.float32)
+        total = term if total is None else total + term
     out[...] = (total.T + out_bias_v[...]).astype(out.dtype)
 
     bytes_of(conv_in.at[pl.ds(0, tm_count - 1)], conv_send.at[0])
@@ -513,20 +537,20 @@
         out_specs=pl.BlockSpec(memory_space=pltpu.VMEM),
         scratch_shapes=[
             vmem((halo + steps, width), jnp.bfloat16),
-            vmem((3, width, channels), jnp.bfloat16),
+            vmem((width, 3 * channels), jnp.bfloat16),
             vmem(proj_bias.shape, jnp.float32),
             vmem(short_taps.shape, jnp.float32),
             vmem(short_bias.shape, jnp.float32),
             vmem((2, 2, steps, channels), jnp.float32),
             vmem((1, channels), jnp.float32),
             vmem((width, channels), jnp.bfloat16),
-            vmem((2, chan_count, channels, channels // 2), jnp.bfloat16),
+            vmem((2, channels, width // 2), jnp.bfloat16),
             vmem((1, channels), jnp.float32),
             vmem(dft.shape, jnp.bfloat16),
             vmem(twist.shape, jnp.float32),
             vmem((3, halo + steps, channels), jnp.float32),
-            vmem((tm_count, 2, 2, share, steps), jnp.bfloat16),
-            vmem((tm_count, 2, 2, share, steps), jnp.bfloat16),
+            vmem((2, tm_count, 2, share, steps), jnp.bfloat16),
+            vmem((2, tm_count, 2, share, steps), jnp.bfloat16),
             vmem(spread_shape, jnp.bfloat16),
             vmem(spread_shape, jnp.bfloat16),
             vmem((2, tm_count + 1, share, steps), jnp.bfloat16),
@@ -535,13 +559,16 @@
             vmem(spread_shape, jnp.float32),
             vmem(spread_shape, jnp.float32),
             vmem((2, chan_count, channels // 2, steps), jnp.bfloat16),
-            dma((len(operands),)),
-            *[dma((2,))] * 12,
+            dma((len(operands) + 2,)),
+            dma((1,)),
+            dma((4,)),
+            *[dma((2,))] * 9,
+            dma((2, 3)),
         ],
         compiler_params=pltpu.CompilerParams(
-            collective_id=0, has_side_effects=True, vmem_limit_bytes=60 * 1024 * 1024
+            collective_id=0, has_side_effects=True, vmem_limit_bytes=32 * 1024 * 1024
         ),
-    )(*operands)
+    )(*[pltpu.with_memory_space_constraint(operand, pltpu.HBM) for operand in operands])
 
 
 def solution(mesh):
@@ -549,8 +576,8 @@
 
     def program(*arrays):
         share = arrays[0].shape[1] // sizes["chan"] // sizes["tm"]
-        wide = share > 0 and share % 16 == 0 and sizes["tm"] >= 4
-        wide = wide and all(size & size - 1 == 0 for size in sizes.values())
+        wide = share > 0 and share % 16 == 0 and sizes["tm"] >= 4 and sizes["chan"] == 4
+        wide = wide and sizes["tm"] & sizes["tm"] - 1 == 0
         return jax.shard_map(
             fused if wide else shards,
             mesh=mesh,

time: 28 us -> 25.7 us (0.918)
  Pallas kernels: 26.3 us -> 24.8 us
  local copies, waits for them, and re-layouts: 1.47 us -> 0.63 us
    pallas_call x1, Pallas kernels: 26.3 us -> 24.8 us  [fused(): pl.pallas_call(functools.partial(kernel, tm_count, chan_count), out_shape...]
    unnamed x1, local copies, waits for them, and re-layouts: 1.47 us -> 0.63 us
where the time goes in v4:
time: 25.7 us; the launch traced here: 25.4 us
  Pallas kernels  24.8 us (96%)
  local copies, waits for them, and re-layouts  0.63 us (2%)
    pallas_call x1, Pallas kernels, fused(): pl.pallas_call(functools.partial(kernel, tm_count, chan_count), out_shape...  24.8 us
    unnamed x1, local copies, waits for them, and re-layouts  0.63 us

profile of v4, /device:TPU:0, one launch (start us, length us, event | category | flops | bytes accessed | tf_op | source)
XLA Modules:
  0.0 25.4 jit_solution(8368782509781138699)
XLA Ops:
  0.0 24.8 %shard_map.109 = bf16[256,128]{1,0:T(8,128)(2,1)S(1)} custom-call(bf16[256,128]{1,0:T(8,128)(2,1)} %series.1, bf16[3,512,128]{2,1,0:T(8,128)(2,1)} %bitcast.3, f32[3,128]{1,0:T(4,128)} %proj_bias.1, f32[3,3,128]{2,1,0:T(4,128)} %taps.1, f32[3,128]{1,0:T(4,128)} %short_bias.1, f32[2,1,2,256,128]{4,3,2,1,0:T(8,128)} %spectrum.1, f32[1,128]{1,0:T(1,128)} %bitcast.4, ...), custom_call_target="tpu_custom_call" | custom-call | tf_op jit(solution)/shard_map/pallas_call | solution.py:533
  24.8 0.6 %copy.13 = bf16[256,128]{1,0:T(8,128)(2,1)} copy(bf16[256,128]{1,0:T(8,128)(2,1)S(1)} %shard_map.109) | data formatting | bytes 131072

commit v5 on v4

--- a/solution.py
+++ b/solution.py
@@ -263,7 +263,7 @@
     pairs = [
         (series, rows_in.at[pl.ds(halo, steps), columns(own_c)]),
         (spectrum.at[:, 0], spectrum_v),
-        *[(weight.at[j], weight_v.at[:, pl.ds(j * channels, channels)]) for j in range(3)],
+        *[(weight.at[j], weight_v.at[:, pl.ds((j + 2) % 3 * channels, channels)]) for j in range(3)],
         (proj_bias, proj_bias_v),
         (taps, taps_v),
         (short_bias, short_bias_v),
@@ -276,7 +276,6 @@
     local = [pltpu.make_async_copy(a, b, local_sem.at[i]) for i, (a, b) in enumerate(pairs)]
     for copy in local:
         copy.start()
-    own_rows = rows_in.at[pl.ds(halo, steps), columns(own_c)]
 
     def remote(src, dst, send, recv, where):
         return pltpu.make_async_remote_copy(
@@ -295,9 +294,14 @@
             block = jnp.dot(order, block, preferred_element_type=jnp.float32).T
             spec_out[parity, :, part] = block.astype(jnp.bfloat16).reshape(tm_count, share, steps)
 
-    local[1].wait()
-    turn_spectrum(0)
-    local[0].wait()
+    early = own_t < tm_count // 2
+
+    @pl.when(early)
+    def _():
+        local[1].wait()
+        turn_spectrum(0)
+        turn_spectrum(1)
+
     pl.semaphore_wait(barrier, chan_count - 1 + tm_count - 1 + 2 * (chan_count - 1))
 
     core_c, x_c, far_c = chan_peer(1), chan_peer(2), chan_peer(3)
@@ -305,11 +309,12 @@
 
     def rows_copy(owner, first, count, recv, to):
         block = rows_in.at[pl.ds(halo + first, count), columns(owner)]
-        return remote(block, block, rows_send.at[0], rows_recv.at[recv], {"chan": to})
+        source = series.at[pl.ds(first, count)] if owner is own_c else block
+        return remote(source, block, rows_send.at[0], rows_recv.at[recv], {"chan": to})
 
     def halo_copy(by, owner):
         return remote(
-            rows_in.at[pl.ds(steps, halo), columns(own_c)],
+            series.at[pl.ds(steps - halo, halo)],
             rows_in.at[pl.ds(0, halo), columns(owner)],
             halo_send.at[0],
             halo_recv.at[0],
@@ -340,13 +345,26 @@
     def collect(dst, recv):
         bytes_of(dst.at[pl.ds(0, tm_count - 1)], recv)
 
-    spread(spec_out.at[0], spec_in.at[0], spec_send.at[0], spec_recv.at[0])
-    turn_spectrum(1)
-    spread(spec_out.at[1], spec_in.at[1], spec_send.at[1], spec_recv.at[1])
+    def spread_spectrum(parity):
+        spread(spec_out.at[parity], spec_in.at[parity], spec_send.at[parity], spec_recv.at[parity])
+
+    @pl.when(early)
+    def _():
+        spread_spectrum(0)
+        spread_spectrum(1)
+
+    @pl.when(jnp.logical_not(early))
+    def _():
+        local[1].wait()
+        for parity in range(2):
+            turn_spectrum(parity)
+            spread_spectrum(parity)
+
 
     for i in range(2):
         bytes_of(rows_in.at[pl.ds(halo, part_rows), columns(x_c)], rows_recv.at[i])
         rows_copy(x_c, i * part_rows, part_rows, 3, core_c).start()
+    local[0].wait()
     for copy in local[2:]:
         copy.wait()
     others = pl.ds(0, (chan_count - 1) * channels)
@@ -359,7 +377,9 @@
 
     def of_chip(chip):
         inputs = pl.ds(pl.multiple_of(chip * 2 * channels, 2 * channels), 2 * channels)
-        return jnp.dot(rows_in[:, inputs], weight_v[inputs, :], preferred_element_type=jnp.float32)
+        return jnp.dot(
+            rows_in[:, inputs], weight_v[inputs, pl.ds(0, 2 * channels)], preferred_element_type=jnp.float32
+        )
 
     own_chip = lax.div(own_c, 2)
     near_sum = of_chip(own_chip)
@@ -368,7 +388,12 @@
 
     streams = []
     for j in (1, 2, 0):
-        value = sums[:, j * channels : (j + 1) * channels]
+        if j:
+            value = sums[:, (j - 1) * channels : j * channels]
+        else:
+            value = jnp.dot(
+                rows_in[...], weight_v[:, pl.ds(2 * channels, channels)], preferred_element_type=jnp.float32
+            )
         value = (value + proj_bias_v[j : j + 1]).astype(jnp.bfloat16).astype(jnp.float32)
         projected[j] = value
 

time: 25.7 us -> 25.9 us (level)
  no operation moved by 1% of the time
where the time goes in v5:
time: 25.9 us; the launch traced here: 25.6 us
  Pallas kernels  24.9 us (96%)
  local copies, waits for them, and re-layouts  0.63 us (2%)
    pallas_call x1, Pallas kernels, fused(): pl.pallas_call(functools.partial(kernel, tm_count, chan_count), out_shape...  24.9 us
    unnamed x1, local copies, waits for them, and re-layouts  0.63 us

profile of v5, /device:TPU:0, one launch (start us, length us, event | category | flops | bytes accessed | tf_op | source)
XLA Modules:
  0.0 25.6 jit_solution(8161859093684147577)
XLA Ops:
  0.0 24.9 %shard_map.109 = bf16[256,128]{1,0:T(8,128)(2,1)S(1)} custom-call(bf16[256,128]{1,0:T(8,128)(2,1)} %series.1, bf16[3,512,128]{2,1,0:T(8,128)(2,1)} %bitcast.3, f32[3,128]{1,0:T(4,128)} %proj_bias.1, f32[3,3,128]{2,1,0:T(4,128)} %taps.1, f32[3,128]{1,0:T(4,128)} %short_bias.1, f32[2,1,2,256,128]{4,3,2,1,0:T(8,128)} %spectrum.1, f32[1,128]{1,0:T(1,128)} %bitcast.4, ...), custom_call_target="tpu_custom_call" | custom-call | tf_op jit(solution)/shard_map/pallas_call | solution.py:558
  24.9 0.6 %copy.13 = bf16[256,128]{1,0:T(8,128)(2,1)} copy(bf16[256,128]{1,0:T(8,128)(2,1)S(1)} %shard_map.109) | data formatting | bytes 131072

commit v6 on v5

--- a/solution.py
+++ b/solution.py
@@ -216,9 +216,13 @@
     projected,
     spec_out,
     spec_in,
+    odd_out,
+    odd_in,
     mixed_out,
     mixed_in,
     wave,
+    odd_wave,
+    even_sum,
     conv_out,
     conv_in,
     gate_t,
@@ -292,7 +296,11 @@
         for part in range(2):
             block = spectrum_v[part, parity].astype(jnp.bfloat16)
             block = jnp.dot(order, block, preferred_element_type=jnp.float32).T
-            spec_out[parity, :, part] = block.astype(jnp.bfloat16).reshape(tm_count, share, steps)
+            block = block.astype(jnp.bfloat16).reshape(tm_count, share, steps)
+            if parity:
+                odd_out[part] = block
+            else:
+                spec_out[0, :, part] = block
 
     early = own_t < tm_count // 2
 
@@ -345,8 +353,11 @@
     def collect(dst, recv):
         bytes_of(dst.at[pl.ds(0, tm_count - 1)], recv)
 
-    def spread_spectrum(parity):
-        spread(spec_out.at[parity], spec_in.at[parity], spec_send.at[parity], spec_recv.at[parity])
+    def spread_spectrum(piece):
+        if piece == 0:
+            spread(spec_out.at[0], spec_in.at[0], spec_send.at[0], spec_recv.at[0])
+        else:
+            spread(odd_out.at[piece - 1], odd_in.at[piece - 1], spec_send.at[piece], spec_recv.at[piece])
 
     @pl.when(early)
     def _():
@@ -359,7 +370,6 @@
         for parity in range(2):
             turn_spectrum(parity)
             spread_spectrum(parity)
-
 
     for i in range(2):
         bytes_of(rows_in.at[pl.ds(halo, part_rows), columns(x_c)], rows_recv.at[i])
@@ -409,6 +419,7 @@
             signal = (streams[0] * stream).astype(jnp.bfloat16).astype(jnp.float32)
             mixed_out[...] = signal.T.astype(jnp.bfloat16).reshape(tm_count, share, steps)
             spread(mixed_out, mixed_in, mix_send.at[0], mix_recv.at[0])
+            spread_spectrum(2)
         streams.append(stream)
     gate_t[...] = streams[2].T.reshape(tm_count, share, steps)
     direct_t[...] = (skip_v[...] * signal).T.reshape(tm_count, share, steps)
@@ -427,6 +438,7 @@
     cosine = lambda r, b: math.cos(turns[r * b % slots])
     sine = lambda r, b: math.sin(turns[r * b % slots])
     kept = tm_count + 1
+    waves = (wave, odd_wave)
 
     for r in range(kept):
         real = weighted(blocks, [cosine(r, b) for b in range(tm_count)])
@@ -437,43 +449,53 @@
         else:
             turned = (real * cos_row + imag * sin_row, imag * cos_row - real * sin_row)
         for part in range(2):
-            wave[part, r] = turned[part].astype(jnp.bfloat16)
-
-    def within():
-        rows = wave[...].reshape(2 * kept * share, steps)
+            waves[r % 2][part, r // 2] = turned[part].astype(jnp.bfloat16)
+
+    def within(parity):
+        count = waves[parity].shape[1]
+        rows = waves[parity][...].reshape(2 * count * share, steps)
         first = jnp.dot(rows, dft_v[0], preferred_element_type=jnp.float32)
         second = jnp.dot(rows, dft_v[1], preferred_element_type=jnp.float32)
-        half = kept * share
-        return [a.reshape(kept, share, steps) for a in (first[:half], first[half:], second[:half], second[half:])]
-
-    real_cos, imag_cos, real_sin, imag_sin = within()
-    real, imag = real_cos + imag_sin, imag_cos - real_sin
+        half = count * share
+        return [a.reshape(count, share, steps) for a in (first[:half], first[half:], second[:half], second[half:])]
+
+    def filter_of(part, r):
+        slot = flip(r // 2, digits)
+        return (odd_in[part, slot] if r % 2 else spec_in[0, slot, part]).astype(jnp.float32)
+
+    forward = []
     for parity in range(2):
-        collect(spec_in.at[parity], spec_recv.at[parity])
-
-    def filter_of(part, r):
-        return spec_in[r % 2, flip(r // 2, digits), part].astype(jnp.float32)
-
-    for r in range(kept):
-        filter_real, filter_imag = filter_of(0, r), filter_of(1, r)
-        if 0 < r < tm_count:
-            filter_real = filter_real + filter_of(0, slots - r)
-            filter_imag = filter_imag - filter_of(1, slots - r)
-        wave[0, r] = (real[r] * filter_real - imag[r] * filter_imag).astype(jnp.bfloat16)
-        wave[1, r] = (real[r] * filter_imag + imag[r] * filter_real).astype(jnp.bfloat16)
-    real_cos, imag_cos, real_sin, imag_sin = within()
-    real, imag = real_cos - imag_sin, real_sin + imag_cos
-
-    terms = []
-    for r in range(kept):
-        cos_row, sin_row = twist_v[0, r : r + 1], twist_v[1, r : r + 1]
-        terms.append(real[r] * cos_row - imag[r] * sin_row)
-    for r in range(kept):
-        cos_row, sin_row = twist_v[0, r : r + 1], twist_v[1, r : r + 1]
-        terms.append(real[r] * sin_row + imag[r] * cos_row)
-    for b in range(tm_count):
-        weights = [cosine(r, b) for r in range(kept)] + [-sine(r, b) for r in range(kept)]
-        conv_out[b] = weighted(terms, weights).astype(jnp.bfloat16)
+        real_cos, imag_cos, real_sin, imag_sin = within(parity)
+        forward.append((real_cos + imag_sin, imag_cos - real_sin))
+    sums = []
+    for parity in range(2):
+        if parity:
+            for part in range(2):
+                collect(odd_in.at[part], spec_recv.at[1 + part])
+        else:
+            collect(spec_in.at[0], spec_recv.at[0])
+        real, imag = forward[parity]
+        residues = range(parity, kept, 2)
+        for i, r in enumerate(residues):
+            filter_real, filter_imag = filter_of(0, r), filter_of(1, r)
+            if 0 < r < tm_count:
+                filter_real = filter_real + filter_of(0, slots - r)
+                filter_imag = filter_imag - filter_of(1, slots - r)
+            waves[parity][0, i] = (real[i] * filter_real - imag[i] * filter_imag).astype(jnp.bfloat16)
+            waves[parity][1, i] = (real[i] * filter_imag + imag[i] * filter_real).astype(jnp.bfloat16)
+        real_cos, imag_cos, real_sin, imag_sin = within(parity)
+        real, imag = real_cos - imag_sin, real_sin + imag_cos
+        terms = []
+        for i, r in enumerate(residues):
+            cos_row, sin_row = twist_v[0, r : r + 1], twist_v[1, r : r + 1]
+            terms.append(real[i] * cos_row - imag[i] * sin_row)
+            terms.append(real[i] * sin_row + imag[i] * cos_row)
+        for b in range(tm_count):
+            total = weighted(terms, [w for r in residues for w in (cosine(r, b), -sine(r, b))])
+            if parity:
+                conv_out[b] = (even_sum[b] + total).astype(jnp.bfloat16)
+            else:
+                even_sum[b] = total
     for by in far_first:
         half = by // near
         remote(
@@ -486,8 +508,9 @@
     def _():
         bytes_of(rows_in.at[pl.ds(0, halo)], halo_send.at[0])
 
-    for parity in range(2):
-        collect(spec_in.at[parity], spec_send.at[parity])
+    collect(spec_in.at[0], spec_send.at[0])
+    for part in range(2):
+        collect(odd_in.at[part], spec_send.at[1 + part])
     bytes_of(mixed_in.at[pl.ds(0, tm_count - 1)], mix_send.at[0])
 
     def gate_copy(half, owner, recv, to):
@@ -574,11 +597,15 @@
             vmem(dft.shape, jnp.bfloat16),
             vmem(twist.shape, jnp.float32),
             vmem((3, halo + steps, channels), jnp.float32),
-            vmem((2, tm_count, 2, share, steps), jnp.bfloat16),
-            vmem((2, tm_count, 2, share, steps), jnp.bfloat16),
+            vmem((1, tm_count, 2, share, steps), jnp.bfloat16),
+            vmem((1, tm_count, 2, share, steps), jnp.bfloat16),
+            vmem((2, *spread_shape), jnp.bfloat16),
+            vmem((2, *spread_shape), jnp.bfloat16),
             vmem(spread_shape, jnp.bfloat16),
             vmem(spread_shape, jnp.bfloat16),
-            vmem((2, tm_count + 1, share, steps), jnp.bfloat16),
+            vmem((2, tm_count // 2 + 1, share, steps), jnp.bfloat16),
+            vmem((2, tm_count // 2, share, steps), jnp.bfloat16),
+            vmem(spread_shape, jnp.float32),
             vmem(spread_shape, jnp.bfloat16),
             vmem(spread_shape, jnp.bfloat16),
             vmem(spread_shape, jnp.float32),
@@ -587,7 +614,7 @@
             dma((len(operands) + 2,)),
             dma((1,)),
             dma((4,)),
-            *[dma((2,))] * 9,
+            *[dma((3,))] * 9,
             dma((2, 3)),
         ],
         compiler_params=pltpu.CompilerParams(

time: 25.9 us -> 26.6 us (1.027)
  Pallas kernels: 24.9 us -> 25.6 us
    pallas_call x1, Pallas kernels: 24.9 us -> 25.6 us  [fused(): pl.pallas_call(functools.partial(kernel, tm_count, chan_count), out_shape...]
where the time goes in v6:
time: 26.6 us; the launch traced here: 26.2 us
  Pallas kernels  25.6 us (96%)
  local copies, waits for them, and re-layouts  0.63 us (2%)
    pallas_call x1, Pallas kernels, fused(): pl.pallas_call(functools.partial(kernel, tm_count, chan_count), out_shape...  25.6 us
    unnamed x1, local copies, waits for them, and re-layouts  0.63 us

profile of v6, /device:TPU:0, one launch (start us, length us, event | category | flops | bytes accessed | tf_op | source)
XLA Modules:
  0.0 26.2 jit_solution(2869534774316213874)
XLA Ops:
  0.0 25.6 %shard_map.109 = bf16[256,128]{1,0:T(8,128)(2,1)S(1)} custom-call(bf16[256,128]{1,0:T(8,128)(2,1)} %series.1, bf16[3,512,128]{2,1,0:T(8,128)(2,1)} %bitcast.3, f32[3,128]{1,0:T(4,128)} %proj_bias.1, f32[3,3,128]{2,1,0:T(4,128)} %taps.1, f32[3,128]{1,0:T(4,128)} %short_bias.1, f32[2,1,2,256,128]{4,3,2,1,0:T(8,128)} %spectrum.1, f32[1,128]{1,0:T(1,128)} %bitcast.4, ...), custom_call_target="tpu_custom_call" | custom-call | tf_op jit(solution)/shard_map/pallas_call | solution.py:581
  25.6 0.6 %copy.13 = bf16[256,128]{1,0:T(8,128)(2,1)} copy(bf16[256,128]{1,0:T(8,128)(2,1)S(1)} %shard_map.109) | data formatting | bytes 131072

commit v7 on v5

--- a/solution.py
+++ b/solution.py
@@ -291,7 +291,9 @@
         order = jnp.where(wanted == across, 1.0 / (slots * steps), 0.0).astype(jnp.bfloat16)
         for part in range(2):
             block = spectrum_v[part, parity].astype(jnp.bfloat16)
-            block = jnp.dot(order, block, preferred_element_type=jnp.float32).T
+            block = lax.dot_general(
+                block, order, (((0,), (0,)), ((), ())), preferred_element_type=jnp.float32
+            )
             spec_out[parity, :, part] = block.astype(jnp.bfloat16).reshape(tm_count, share, steps)
 
     early = own_t < tm_count // 2
@@ -345,6 +347,11 @@
     def collect(dst, recv):
         bytes_of(dst.at[pl.ds(0, tm_count - 1)], recv)
 
+    def relay_rows():
+        for i in range(2):
+            bytes_of(rows_in.at[pl.ds(halo, part_rows), columns(x_c)], rows_recv.at[i])
+            rows_copy(x_c, i * part_rows, part_rows, 3, core_c).start()
+
     def spread_spectrum(parity):
         spread(spec_out.at[parity], spec_in.at[parity], spec_send.at[parity], spec_recv.at[parity])
 
@@ -352,18 +359,17 @@
     def _():
         spread_spectrum(0)
         spread_spectrum(1)
+        relay_rows()
 
     @pl.when(jnp.logical_not(early))
     def _():
         local[1].wait()
-        for parity in range(2):
-            turn_spectrum(parity)
-            spread_spectrum(parity)
-
-
-    for i in range(2):
-        bytes_of(rows_in.at[pl.ds(halo, part_rows), columns(x_c)], rows_recv.at[i])
-        rows_copy(x_c, i * part_rows, part_rows, 3, core_c).start()
+        turn_spectrum(0)
+        spread_spectrum(0)
+        relay_rows()
+        turn_spectrum(1)
+        spread_spectrum(1)
+
     local[0].wait()
     for copy in local[2:]:
         copy.wait()

time: 25.9 us -> 25.9 us (level)
  no operation moved by 1% of the time
where the time goes in v7:
time: 25.9 us; the launch traced here: 25.6 us
  Pallas kernels  24.9 us (96%)
  local copies, waits for them, and re-layouts  0.63 us (2%)
    pallas_call x1, Pallas kernels, fused(): pl.pallas_call(functools.partial(kernel, tm_count, chan_count), out_shape...  24.9 us
    unnamed x1, local copies, waits for them, and re-layouts  0.63 us

profile of v7, /device:TPU:0, one launch (start us, length us, event | category | flops | bytes accessed | tf_op | source)
XLA Modules:
  0.0 25.6 jit_solution(8654216263912311134)
XLA Ops:
  0.0 24.9 %shard_map.109 = bf16[256,128]{1,0:T(8,128)(2,1)S(1)} custom-call(bf16[256,128]{1,0:T(8,128)(2,1)} %series.1, bf16[3,512,128]{2,1,0:T(8,128)(2,1)} %bitcast.3, f32[3,128]{1,0:T(4,128)} %proj_bias.1, f32[3,3,128]{2,1,0:T(4,128)} %taps.1, f32[3,128]{1,0:T(4,128)} %short_bias.1, f32[2,1,2,256,128]{4,3,2,1,0:T(8,128)} %spectrum.1, f32[1,128]{1,0:T(1,128)} %bitcast.4, ...), custom_call_target="tpu_custom_call" | custom-call | tf_op jit(solution)/shard_map/pallas_call | solution.py:564
  24.9 0.6 %copy.13 = bf16[256,128]{1,0:T(8,128)(2,1)} copy(bf16[256,128]{1,0:T(8,128)(2,1)S(1)} %shard_map.109) | data formatting | bytes 131072

commit v8 on v7

--- a/solution.py
+++ b/solution.py
@@ -274,8 +274,7 @@
         (out_bias, out_bias_v),
     ]
     local = [pltpu.make_async_copy(a, b, local_sem.at[i]) for i, (a, b) in enumerate(pairs)]
-    for copy in local:
-        copy.start()
+    local[1].start()
 
     def remote(src, dst, send, recv, where):
         return pltpu.make_async_remote_copy(
@@ -325,6 +324,7 @@
 
     for i in range(2):
         rows_copy(own_c, i * part_rows, part_rows, i, x_c).start()
+    rows_copy(own_c, part_rows, part_rows, 3, far_c).start()
     rows_copy(own_c, 0, steps, 2, core_c).start()
 
     @pl.when(own_t < tm_count - 1)
@@ -347,10 +347,12 @@
     def collect(dst, recv):
         bytes_of(dst.at[pl.ds(0, tm_count - 1)], recv)
 
+    for copy in local[:1] + local[2:]:
+        copy.start()
+
     def relay_rows():
-        for i in range(2):
-            bytes_of(rows_in.at[pl.ds(halo, part_rows), columns(x_c)], rows_recv.at[i])
-            rows_copy(x_c, i * part_rows, part_rows, 3, core_c).start()
+        bytes_of(rows_in.at[pl.ds(halo, part_rows), columns(x_c)], rows_recv.at[0])
+        rows_copy(x_c, 0, part_rows, 4, core_c).start()
 
     def spread_spectrum(parity):
         spread(spec_out.at[parity], spec_in.at[parity], spec_send.at[parity], spec_recv.at[parity])
@@ -389,7 +391,9 @@
 
     own_chip = lax.div(own_c, 2)
     near_sum = of_chip(own_chip)
-    bytes_of(rows_in.at[pl.ds(halo, steps), columns(far_c)], rows_recv.at[3])
+    bytes_of(rows_in.at[pl.ds(halo, part_rows), columns(x_c)], rows_recv.at[1])
+    for i in range(2):
+        bytes_of(rows_in.at[pl.ds(halo, part_rows), columns(far_c)], rows_recv.at[3 + i])
     sums = near_sum + of_chip(1 - own_chip)
 
     streams = []
@@ -511,14 +515,18 @@
             value = (arrived.astype(jnp.float32) + direct_t[source]) * gate_t[source]
             gated[half, own_c, pl.ds(by % near * share, share)] = value.astype(jnp.bfloat16)
         gate_copy(half, own_c, 0, x_c).start()
+        if half:
+            gate_copy(half, own_c, 2, far_c).start()
         gate_copy(half, own_c, 1, core_c).start()
-    for half in range(2):
-        bytes_of(gated.at[half, x_c], gate_recv.at[half, 0])
-        gate_copy(half, x_c, 2, core_c).start()
+
+    bytes_of(gated.at[0, x_c], gate_recv.at[0, 0])
+    gate_copy(0, x_c, 2, core_c).start()
 
     total = None
     for half in range(2):
         bytes_of(gated.at[half, core_c], gate_recv.at[half, 1])
+        if half:
+            bytes_of(gated.at[half, x_c], gate_recv.at[half, 0])
         bytes_of(gated.at[half, far_c], gate_recv.at[half, 2])
         rows = gated[half].reshape(chan_count * channels // 2, steps)
         term = jnp.dot(out_weight_t[half], rows, preferred_element_type=jnp.float32)
@@ -592,7 +600,7 @@
             vmem((2, chan_count, channels // 2, steps), jnp.bfloat16),
             dma((len(operands) + 2,)),
             dma((1,)),
-            dma((4,)),
+            dma((5,)),
             *[dma((2,))] * 9,
             dma((2, 3)),
         ],

time: 25.9 us -> 25.4 us (0.981)
  Pallas kernels: 24.9 us -> 24.6 us
    pallas_call x1, Pallas kernels: 24.9 us -> 24.6 us  [fused(): pl.pallas_call(functools.partial(kernel, tm_count, chan_count), out_shape...]
where the time goes in v8:
time: 25.4 us; the launch traced here: 25.3 us
  Pallas kernels  24.6 us (97%)
  local copies, waits for them, and re-layouts  0.63 us (2%)
    pallas_call x1, Pallas kernels, fused(): pl.pallas_call(functools.partial(kernel, tm_count, chan_count), out_shape...  24.6 us
    unnamed x1, local copies, waits for them, and re-layouts  0.63 us

profile of v8, /device:TPU:0, one launch (start us, length us, event | category | flops | bytes accessed | tf_op | source)
XLA Modules:
  0.0 25.3 jit_solution(9716258253866843243)
XLA Ops:
  0.0 24.6 %shard_map.109 = bf16[256,128]{1,0:T(8,128)(2,1)S(1)} custom-call(bf16[256,128]{1,0:T(8,128)(2,1)} %series.1, bf16[3,512,128]{2,1,0:T(8,128)(2,1)} %bitcast.3, f32[3,128]{1,0:T(4,128)} %proj_bias.1, f32[3,3,128]{2,1,0:T(4,128)} %taps.1, f32[3,128]{1,0:T(4,128)} %short_bias.1, f32[2,1,2,256,128]{4,3,2,1,0:T(8,128)} %spectrum.1, f32[1,128]{1,0:T(1,128)} %bitcast.4, ...), custom_call_target="tpu_custom_call" | custom-call | tf_op jit(solution)/shard_map/pallas_call | solution.py:572
  24.7 0.6 %copy.13 = bf16[256,128]{1,0:T(8,128)(2,1)} copy(bf16[256,128]{1,0:T(8,128)(2,1)S(1)} %shard_map.109) | data formatting | bytes 131072

commit v9 on v8

--- a/solution.py
+++ b/solution.py
@@ -290,9 +290,7 @@
         order = jnp.where(wanted == across, 1.0 / (slots * steps), 0.0).astype(jnp.bfloat16)
         for part in range(2):
             block = spectrum_v[part, parity].astype(jnp.bfloat16)
-            block = lax.dot_general(
-                block, order, (((0,), (0,)), ((), ())), preferred_element_type=jnp.float32
-            )
+            block = jnp.dot(order, block, preferred_element_type=jnp.float32).T
             spec_out[parity, :, part] = block.astype(jnp.bfloat16).reshape(tm_count, share, steps)
 
     early = own_t < tm_count // 2
@@ -366,11 +364,10 @@
     @pl.when(jnp.logical_not(early))
     def _():
         local[1].wait()
-        turn_spectrum(0)
-        spread_spectrum(0)
+        for parity in range(2):
+            turn_spectrum(parity)
+            spread_spectrum(parity)
         relay_rows()
-        turn_spectrum(1)
-        spread_spectrum(1)
 
     local[0].wait()
     for copy in local[2:]:

time: 25.4 us -> 25.4 us (level)
  no operation moved by 1% of the time
where the time goes in v9:
time: 25.4 us; the launch traced here: 25.3 us
  Pallas kernels  24.6 us (97%)
  local copies, waits for them, and re-layouts  0.63 us (2%)
    pallas_call x1, Pallas kernels, fused(): pl.pallas_call(functools.partial(kernel, tm_count, chan_count), out_shape...  24.6 us
    unnamed x1, local copies, waits for them, and re-layouts  0.63 us

profile of v9, /device:TPU:0, one launch (start us, length us, event | category | flops | bytes accessed | tf_op | source)
XLA Modules:
  0.0 25.3 jit_solution(14527993108674416647)
XLA Ops:
  0.0 24.6 %shard_map.109 = bf16[256,128]{1,0:T(8,128)(2,1)S(1)} custom-call(bf16[256,128]{1,0:T(8,128)(2,1)} %series.1, bf16[3,512,128]{2,1,0:T(8,128)(2,1)} %bitcast.3, f32[3,128]{1,0:T(4,128)} %proj_bias.1, f32[3,3,128]{2,1,0:T(4,128)} %taps.1, f32[3,128]{1,0:T(4,128)} %short_bias.1, f32[2,1,2,256,128]{4,3,2,1,0:T(8,128)} %spectrum.1, f32[1,128]{1,0:T(1,128)} %bitcast.4, ...), custom_call_target="tpu_custom_call" | custom-call | tf_op jit(solution)/shard_map/pallas_call | solution.py:569
  24.7 0.6 %copy.13 = bf16[256,128]{1,0:T(8,128)(2,1)} copy(bf16[256,128]{1,0:T(8,128)(2,1)S(1)} %shard_map.109) | data formatting | bytes 131072

commit v10 on v9

--- a/solution.py
+++ b/solution.py
@@ -512,18 +512,14 @@
             value = (arrived.astype(jnp.float32) + direct_t[source]) * gate_t[source]
             gated[half, own_c, pl.ds(by % near * share, share)] = value.astype(jnp.bfloat16)
         gate_copy(half, own_c, 0, x_c).start()
-        if half:
-            gate_copy(half, own_c, 2, far_c).start()
+        gate_copy(half, own_c, 2, far_c).start()
         gate_copy(half, own_c, 1, core_c).start()
 
-    bytes_of(gated.at[0, x_c], gate_recv.at[0, 0])
-    gate_copy(0, x_c, 2, core_c).start()
 
     total = None
     for half in range(2):
         bytes_of(gated.at[half, core_c], gate_recv.at[half, 1])
-        if half:
-            bytes_of(gated.at[half, x_c], gate_recv.at[half, 0])
+        bytes_of(gated.at[half, x_c], gate_recv.at[half, 0])
         bytes_of(gated.at[half, far_c], gate_recv.at[half, 2])
         rows = gated[half].reshape(chan_count * channels // 2, steps)
         term = jnp.dot(out_weight_t[half], rows, preferred_element_type=jnp.float32)

time: 25.4 us -> 25.4 us (level)
  no operation moved by 1% of the time
where the time goes in v10:
time: 25.4 us; the launch traced here: 25.3 us
  Pallas kernels  24.6 us (97%)
  local copies, waits for them, and re-layouts  0.63 us (2%)
    pallas_call x1, Pallas kernels, fused(): pl.pallas_call(functools.partial(kernel, tm_count, chan_count), out_shape...  24.6 us
    unnamed x1, local copies, waits for them, and re-layouts  0.63 us

profile of v10, /device:TPU:0, one launch (start us, length us, event | category | flops | bytes accessed | tf_op | source)
XLA Modules:
  0.0 25.3 jit_solution(9508310426378910009)
XLA Ops:
  0.0 24.6 %shard_map.109 = bf16[256,128]{1,0:T(8,128)(2,1)S(1)} custom-call(bf16[256,128]{1,0:T(8,128)(2,1)} %series.1, bf16[3,512,128]{2,1,0:T(8,128)(2,1)} %bitcast.3, f32[3,128]{1,0:T(4,128)} %proj_bias.1, f32[3,3,128]{2,1,0:T(4,128)} %taps.1, f32[3,128]{1,0:T(4,128)} %short_bias.1, f32[2,1,2,256,128]{4,3,2,1,0:T(8,128)} %spectrum.1, f32[1,128]{1,0:T(1,128)} %bitcast.4, ...), custom_call_target="tpu_custom_call" | custom-call | tf_op jit(solution)/shard_map/pallas_call | solution.py:565
  24.7 0.6 %copy.13 = bf16[256,128]{1,0:T(8,128)(2,1)} copy(bf16[256,128]{1,0:T(8,128)(2,1)S(1)} %shard_map.109) | data formatting | bytes 131072
